TPU v7x, 512 devices: a whole 4x8x8 slice. The times are simulated.
512 devices in a mesh: dp: 32 (over x_hi, y, core), ctx: 16 (over z, x_lo).
Axes of the slice: x: 4 (x_hi: 2, x_lo: 2; x = x_hi * 2 + x_lo), y: 8, z: 8, core: 2. Of those that a mesh axis runs over, the one named last changes fastest.
Arguments:
- inputs: bfloat16 [65536, 8192], P(('dp', 'ctx')), may hold values from -8 to 8
- key_output_gradient: bfloat16 [65536, 640], P(('dp', 'ctx')), may hold values from -240 to 240
- frozen_key_weight: bfloat16 [8192, 640], P('dp'), may hold values from -0.0625 to 0.0625
- adapter_first_factor: bfloat16 [8192, 64], P('dp'), may hold values from -0.0625 to 0.0625
- adapter_second_factor: bfloat16 [64, 640], replicated, may hold values from -0.75 to 0.75
- privacy_noise_first: float32 [8192, 64], P('ctx'), may hold values from -6 to 6
- privacy_noise_second: float32 [64, 640], P(None, 'ctx'), may hold values from -6 to 6
Outputs:
- d_input: bfloat16 [65536, 8192], P(('dp', 'ctx'))
- grad_a: float32 [8192, 64], P('ctx')
- grad_b: float32 [64, 640], P(None, 'ctx')
All inputs are finite; a program needn't handle non-finite values.
Results may differ from a plain program's by a relative error of at most 0.014.
Values may be sent and summed in bfloat16 or wider, within the bound.
No kernel may reach another device: no remote copies, remote signals or barrier semaphores. Data moves between devices by JAX's collectives and lax.ppermute only.
A program may use at most 64 MiB of HBM per device.

v0:
```python
import jax
import jax.numpy as jnp
from jax import lax
from jax.sharding import PartitionSpec as P

ADAPTER_SCALE = 2.0
NOISE = 0.005


def per_device(
    inputs,
    key_output_gradient,
    frozen_key_weight,
    adapter_first_factor,
    adapter_second_factor,
    privacy_noise_first,
    privacy_noise_second,
):
    lowrank_gradient = (
        ADAPTER_SCALE
        * jnp.dot(key_output_gradient, adapter_second_factor.T, preferred_element_type=jnp.float32)
    ).astype(jnp.bfloat16)
    w_piece = lax.all_gather(frozen_key_weight, "dp", axis=0, tiled=True)
    first_factor_slice = lax.all_gather(adapter_first_factor, "dp", axis=0, tiled=True)
    columns = jnp.dot(key_output_gradient, w_piece.T, preferred_element_type=jnp.float32) + jnp.dot(
        lowrank_gradient, first_factor_slice.T, preferred_element_type=jnp.float32
    )
    grad_full = columns
    low_full = jnp.dot(inputs, first_factor_slice, preferred_element_type=jnp.float32)
    grad_full, low_full = (grad_full, low_full)
    d_input = grad_full.astype(jnp.bfloat16)
    hidden_lowrank = low_full.astype(jnp.bfloat16)
    part_a = jnp.einsum("td,tr->dr", inputs, lowrank_gradient, preferred_element_type=jnp.float32)
    part_b = ADAPTER_SCALE * jnp.einsum(
        "tr,tk->rk", hidden_lowrank, key_output_gradient, preferred_element_type=jnp.float32
    )
    doc_count = lax.axis_size("dp")
    total_a, total_b = (
        lax.psum(part_a.astype(jnp.bfloat16), "ctx").astype(jnp.float32),
        lax.psum(part_b.astype(jnp.bfloat16), "ctx").astype(jnp.float32),
    )
    norm_doc = jnp.sqrt(jnp.sum(total_a * total_a) + jnp.sum(total_b * total_b))
    bound = lax.psum(norm_doc, "dp") / doc_count
    ctx_place = lax.axis_index("ctx")
    row_count = total_a.shape[0] // lax.axis_size("ctx")
    col_count = total_b.shape[1] // lax.axis_size("ctx")
    share_a = lax.dynamic_slice_in_dim(total_a, ctx_place * row_count, row_count, 0)
    share_b = lax.dynamic_slice_in_dim(total_b, ctx_place * col_count, col_count, 1)
    factor = bound / jnp.maximum(norm_doc, bound)
    sum_a, sum_b = lax.psum((factor * share_a, factor * share_b), "dp")
    grad_a = (sum_a + NOISE * bound * privacy_noise_first) / doc_count
    grad_b = (sum_b + NOISE * bound * privacy_noise_second) / doc_count
    return (d_input, grad_a, grad_b)


def solution(mesh):
    return jax.shard_map(
        per_device,
        mesh=mesh,
        in_specs=(
            P(("dp", "ctx"), None),
            P(("dp", "ctx"), None),
            P("dp", None),
            P("dp", None),
            P(),
            P("ctx", None),
            P(None, "ctx"),
        ),
        out_specs=(P(("dp", "ctx"), None), P("ctx", None), P(None, "ctx")),
        check_vma=False,
    )
```

profile of v0, /device:TPU:1, one launch (start us, length us, event | category | flops | bytes accessed | tf_op | source)
XLA Modules:
  0.0 692.8 jit_solution(11711050096838156126)
XLA Ops:
  7.2 0.0 copy-start
  7.2 0.0 copy-start.2
  7.2 0.0 all-gather.5.cloned.1.call-start
  7.2 0.7 all-gather.5.cloned.1.call-update
  7.9 0.0 all-reduce.6.cloned.1.call-start
  8.0 1.1 fusion.3
  9.1 0.0 copy-done
  9.1 1.4 fusion.1
  10.5 83.9 %all-gather.5.cloned.1.call-done = bf16[8192,64]{0,1:T(8,128)(2,1)} async-done(((bf16[256,64]{0,1:T(8,128)(2,1)}), bf16[8192,64]{0,1:T(8,128)(2,1)}) %all-gather.5.cloned.1.call-update) | async-done | bytes 1048592 | tf_op jit(solution)/shard_map/all_gather | solution.py:24
  94.4 0.0 copy-done.2
  94.4 2.8 fusion.2
  97.2 0.0 all-reduce.6.cloned.1.call-update
  97.2 0.0 all-reduce.4.cloned.1.call-start
  97.3 135.6 %all-reduce.6.cloned.1.call-done = (bf16[8192,64]{0,1:T(8,128)(2,1)}, bf16[64,640]{1,0:T(8,128)(2,1)}) async-done(((bf16[8192,64]{0,1:T(8,128)(2,1)}, bf16[64,640]{1,0:T(8,128)(2,1)}), (bf16[8192,64]{0,1:T(8,128)(2,1)}, bf16[64,640]{1,0:T(8,128)(2,1)})) %all-reduce.6.cloned.1.call-update) | async-done | bytes 1130512 | tf_op jit(solution)/shard_map/psum | solution.py:39
  232.8 2.4 multiply_reduce_fusion
  235.2 0.0 copy-start.5
  235.2 0.0 copy-start.3
  235.2 1.6 multiply_reduce_fusion.1
  238.1 0.0 copy-start.4
  238.2 2.7 convert_element_type.28
  240.9 75.0 %psum.37 = f32[]{:T(128)} all-reduce(f32[]{:T(128)S(6)} %sqrt.3), channel_id=1, replica_groups=mesh['dp'=32,'ctx'=16] {'dp'}, use_global_device_ids=true, to_apply=%region_4.0 | all-reduce | flops 1 | bytes 8 | tf_op jit(solution)/shard_map/psum | solution.py:43
  316.5 1.6 dynamic-slice_multiply_fusion
  318.1 0.0 all-reduce.4.cloned.1.call-update
  318.1 0.0 all-gather.3.cloned.1.call-start
  318.2 0.5 all-gather.3.cloned.1.call-update
  318.7 0.0 copy-done.5
  318.7 0.1 copy.10
  318.8 0.0 copy-done.3
  319.5 0.1 dynamic-slice_multiply_fusion.1
  319.6 123.1 %psum.39 = f32[64,40]{1,0:T(8,128)S(1)} all-reduce(f32[64,40]{1,0:T(8,128)S(1)} %dynamic-slice_multiply_fusion.1), channel_id=1, replica_groups=mesh['dp'=32,'ctx'=16] {'dp'}, use_global_device_ids=true, to_apply=%region_6.0 | all-reduce | flops 2560 | bytes 20480 | tf_op jit(solution)/shard_map/psum | solution.py:50
  442.7 0.7 copy.11
  443.4 116.7 %all-reduce.4.cloned.1.call-done = f32[512,64]{0,1:T(8,128)} async-done(((f32[512,64]{0,1:T(8,128)}), f32[512,64]{0,1:T(8,128)}) %all-reduce.4.cloned.1.call-update) | async-done | bytes 131088 | tf_op jit(solution)/shard_map/psum | solution.py:50
  560.0 0.0 copy-done.4
  560.0 1.6 add_multiply_fusion
  561.6 0.0 copy-start.1
  561.6 115.3 %all-gather.3.cloned.1.call-done = bf16[8192,640]{1,0:T(8,128)(2,1)} async-done(((bf16[256,640]{1,0:T(8,128)(2,1)}), bf16[8192,640]{1,0:T(8,128)(2,1)}) %all-gather.3.cloned.1.call-update) | async-done | bytes 10485776 | tf_op jit(solution)/shard_map/all_gather | solution.py:23
  676.9 7.4 %fusion.4 = f32[128,8192]{1,0:T(8,128)S(1)} fusion(bf16[128,640]{1,0:T(8,128)(2,1)S(1)} %copy-done.2, bf16[8192,640]{1,0:T(8,128)(2,1)} %all-gather.3.cloned.1.call-done), kind=kOutput, calls=%fused_computation.15 | convolution fusion | flops 1342177280 | bytes 14843904 | tf_op jit(solution)/shard_map/dot_general | solution.py:25
  684.2 0.0 copy-done.1
  684.2 2.1 fusion
  (2 shorter events, 0.0 us)
Async XLA Ops:
  7.2 1.9 copy-start
  7.2 87.2 %copy-start.2 = (bf16[128,640]{1,0:T(8,128)(2,1)S(1)}, bf16[128,640]{1,0:T(8,128)(2,1)}, u32[]{:S(2)}) copy-start(bf16[128,640]{1,0:T(8,128)(2,1)} %param.8) | copy-start | bytes 491524
  7.2 87.2 %all-gather.5.cloned.1.call-start = ((), (), s32[]{:S(2)}) async-start(), calls=%async_computation.1 | async-start | bytes 1081344 | tf_op jit(solution)/shard_map/all_gather | solution.py:24
  7.9 224.9 %all-reduce.6.cloned.1.call-start = ((), (), s32[]{:S(2)}) async-start(), calls=%async_computation.3 | async-start | bytes 2260992 | tf_op jit(solution)/shard_map/psum | solution.py:39
  97.2 462.8 %all-reduce.4.cloned.1.call-start = ((), (), s32[]{:S(2)}) async-start(), calls=%async_computation.2 | async-start | bytes 262144 | tf_op jit(solution)/shard_map/psum | solution.py:50
  235.2 83.5 %copy-start.5 = (f32[64,40]{0,1:T(8,128)S(1)}, f32[64,40]{0,1:T(8,128)}, u32[]{:S(2)}) copy-start(f32[64,40]{0,1:T(8,128)} %param.13) | copy-start | bytes 30724
  235.2 83.6 %copy-start.3 = (bf16[64,640]{1,0:T(8,128)(2,1)S(1)}, bf16[64,640]{1,0:T(8,128)(2,1)}, u32[]{:S(2)}) copy-start(bf16[64,640]{1,0:T(8,128)(2,1)} %get-tuple-element.7) | copy-start | bytes 245764
  238.1 321.9 %copy-start.4 = (f32[512,64]{0,1:T(8,128)S(1)}, f32[512,64]{0,1:T(8,128)}, u32[]{:S(2)}) copy-start(f32[512,64]{0,1:T(8,128)} %param.12) | copy-start | bytes 393220
  318.1 358.7 %all-gather.3.cloned.1.call-start = ((), (), s32[]{:S(2)}) async-start(), calls=%async_computation | async-start | bytes 10813440 | tf_op jit(solution)/shard_map/all_gather | solution.py:23
  561.6 122.6 %copy-start.1 = (bf16[8192,64]{0,1:T(8,128)(2,1)S(1)}, bf16[8192,64]{0,1:T(8,128)(2,1)}, u32[]{:S(2)}) copy-start(bf16[8192,64]{0,1:T(8,128)(2,1)} %all-gather.5.cloned.1.call-done) | copy-start | bytes 3145732
Sparse Core Ops, SparseCore 0:
  11.2 83.2 all-gather.4
  98.0 134.7 all-reduce.5
  318.3 241.7 all-reduce.3
  563.8 113.0 all-gather.2
where the time goes:
time: 693 us
  waiting for transfers between devices  453 us (65%)
  blocking collectives  198 us (29%)
  between operations  16.6 us (2%)
  matrix products  14.7 us (2%)
  other arithmetic  9.95 us (1%)
    psum x1, waiting for transfers between devices, per_device(): lax.psum(part_a.astype(jnp.bfloat16), 'ctx').astype(jnp.float32)  136 us
    psum x1, blocking collectives, per_device(): sum_a, sum_b = lax.psum((factor * share_a, factor * share_b), 'dp')  123 us
    psum x1, waiting for transfers between devices, per_device(): sum_a, sum_b = lax.psum((factor * share_a, factor * share_b), 'dp')  117 us
    all_gather x1, waiting for transfers between devices, per_device(): w_piece = lax.all_gather(frozen_key_weight, 'dp', axis=0, tiled=True)  115 us
    all_gather x1, waiting for transfers between devices, per_device(): lax.all_gather(adapter_first_factor, 'dp', axis=0, tiled=True)  83.9 us
    psum x1, blocking collectives, per_device(): bound = lax.psum(norm_doc, 'dp') / doc_count  75 us
  transfers between devices with their start and end apart: 4, of which 4 were waited for; matrix products, arithmetic and copies ran while one was open for 1% of the time, Pallas kernels for 0%

commit v1 on v0

v1 whole, which is shorter than its diff:
```python
import jax
import jax.numpy as jnp
from jax import lax
from jax.experimental import pallas as pl
from jax.experimental.pallas import tpu as pltpu
from jax.sharding import Mesh, PartitionSpec as P

ADAPTER_SCALE = 2.0
NOISE = 0.005
DOCS = 32
CTX = 16
BF16 = jnp.bfloat16
F32 = jnp.float32

PARTS = ("xh", "y", "core", "z", "xl")
PART_SIZES = (2, 8, 2, 8, 2)
DP_PARTS = ("xh", "y", "core")
CTX_PARTS = ("z", "xl")

NT = (((1,), (1,)), ((), ()))
NN = (((1,), (0,)), ((), ()))

SMEM = pl.BlockSpec(memory_space=pltpu.SMEM)
VMEM = pl.BlockSpec(memory_space=pltpu.VMEM)
ANY = pl.BlockSpec(memory_space=pl.ANY)


def dot(a, b, dims):
    return lax.dot_general(a, b, dims, preferred_element_type=F32)


def first_partials_kernel(place_ref, x_ref, g_ref, b_ref, keep_ref, send_ref, order_ref):
    order_ref[...] = jnp.zeros((8, 128), F32)
    u_t = (ADAPTER_SCALE * dot(b_ref[...], g_ref[...], NT)).astype(BF16)
    xl = place_ref[2]
    for ref, at in ((send_ref, 1 - xl), (keep_ref, xl)):
        for z in range(8):
            columns = pl.ds(pl.multiple_of((2 * z + at) * 512, 512), 512)
            ref[z] = dot(u_t, x_ref[:, columns], NN).astype(BF16)


def pair_sum_kernel(a_ref, b_ref, out_ref):
    out_ref[...] = (a_ref[...].astype(F32) + b_ref[...].astype(F32)).astype(BF16)


def second_partials_kernel(place_ref, x_ref, g_ref, own_ref, other_ref, order_ref, msg_ref, gbt_ref, z_ref):
    core = place_ref[0]
    h_t = jnp.zeros((64, 128), F32)
    for block in range(16):
        own_at = pl.multiple_of((2 * block + core) * 256, 256)
        other_at = pl.multiple_of((2 * block + 1 - core) * 256, 256)
        h_t += dot(own_ref[block], x_ref[:, pl.ds(own_at, 256)], NT)
        h_t += dot(other_ref[block], x_ref[:, pl.ds(other_at, 256)], NT)
    gbt_ref[...] = ADAPTER_SCALE * dot(g_ref[...].T, h_t.astype(BF16), NT)
    for q in range(8):
        z_ref[0:80, 64 * q : 64 * q + 64] = gbt_ref[pl.ds(q, 80, stride=8), :]
    z_ref[80:88, :] = jnp.zeros((8, 512), F32)
    keep = lax.broadcasted_iota(jnp.int32, (8, 512), 0) < 5
    for j in range(CTX):
        msg_ref[j] = jnp.where(keep, z_ref[5 * j : 5 * j + 8, :], 0.0).astype(BF16)


def document_share_kernel(first_ref, second_ref, out_ref):
    first = first_ref[0].astype(F32)
    for j in range(1, 8):
        first += first_ref[j].astype(F32)
    second = second_ref[0].astype(F32)
    for j in range(1, CTX):
        second += second_ref[j].astype(F32)
    square = jnp.sum(first * first, axis=0, keepdims=True) + jnp.sum(second * second, axis=0, keepdims=True)
    square = jnp.broadcast_to(jnp.sum(square, axis=1, keepdims=True), (8, 128))
    high = square.astype(BF16).astype(F32)
    middle = (square - high).astype(BF16).astype(F32)
    low = square - high - middle
    row = lax.broadcasted_iota(jnp.int32, (8, 128), 0)
    for k in range(DOCS):
        a, lane = k // 4, 128 * (k % 4)
        tail = jnp.where(row == 1, high, jnp.where(row == 2, middle, jnp.where(row == 3, low, 0.0)))
        tail = jnp.where(row == 0, second[a : a + 1, lane : lane + 128], tail)
        out_ref[k] = jnp.concatenate([first[8 * a : 8 * a + 8, lane : lane + 128], tail], axis=0).astype(BF16)


def squares_kernel(shares_ref, out_ref):
    rows = shares_ref[:, 9, :].astype(F32) + shares_ref[:, 10, :].astype(F32) + shares_ref[:, 11, :].astype(F32)
    group = lax.broadcasted_iota(jnp.int32, (8, 128), 1) // 32
    packed = rows[0:8]
    for at in range(1, 4):
        packed = jnp.where(group == at, rows[8 * at : 8 * at + 8], packed)
    for j in range(CTX):
        out_ref[j] = packed


def clipped_sum_kernel(shares_ref, squares_ref, out_ref):
    squares = squares_ref[0]
    for j in range(1, CTX):
        squares += squares_ref[j]
    norms = jnp.sqrt(
        jnp.concatenate([jnp.broadcast_to(squares[:, 32 * at : 32 * at + 1], (8, 128)) for at in range(4)], axis=0)
    )
    bound = jnp.sum(norms, axis=0, keepdims=True) / DOCS
    factor = bound / jnp.maximum(norms, bound)
    total = factor[0:1] * shares_ref[0].astype(F32)
    for k in range(1, DOCS):
        total += factor[k : k + 1] * shares_ref[k].astype(F32)
    row = lax.broadcasted_iota(jnp.int32, (16, 128), 0)
    total = jnp.where(row == 9, bound, total)
    for k in range(DOCS):
        out_ref[k] = total


def finish_kernel(tiles_ref, noise_a_ref, noise_b_ref, order_ref, grad_a_ref, grad_b_ref, z_ref):
    noise = NOISE * tiles_ref[0, 9:10, 0:1]
    for k in range(DOCS):
        a, lane = 8 * (k // 4), 128 * (k % 4)
        grad_a_ref[a : a + 8, lane : lane + 128] = (
            tiles_ref[k, 0:8, :] + noise * noise_a_ref[a : a + 8, lane : lane + 128]
        ) / DOCS
        z_ref[k // 4 : k // 4 + 1, lane : lane + 128] = tiles_ref[k, 8:9, :]
    for q in range(8):
        at = pl.ds(q, 5, stride=8)
        grad_b_ref[at, :] = (z_ref[0:5, 64 * q : 64 * q + 64] + noise * noise_b_ref[at, :]) / DOCS


def input_gradient_kernel(place_ref, *refs):
    g_refs, (b_ref, at_ref), w_refs, out_refs = refs[0:4], refs[4:6], refs[6:14], refs[14:18]
    g = jnp.concatenate([ref[...] for ref in g_refs], axis=0)
    u = (ADAPTER_SCALE * dot(g, b_ref[...], NT)).astype(BF16)
    for back in range(8):
        y = (place_ref[3] + 8 - back) % 8
        out = (dot(g, w_refs[back][...], NT) + dot(u, at_ref[place_ref[1] * 8 + y], NN)).astype(BF16)
        for at, ref in enumerate(out_refs):
            ref[back] = out[128 * at : 128 * at + 128]


def interleave_kernel(place_ref, *refs):
    own_ref, core_ref, xh_ref, both_ref, out_ref = refs
    core, xh = place_ref[0], place_ref[1]
    for back in range(8):
        y = (place_ref[3] + 8 - back) % 8
        for ref, x_at, core_at in (
            (own_ref, xh, core),
            (core_ref, xh, 1 - core),
            (xh_ref, 1 - xh, core),
            (both_ref, 1 - xh, 1 - core),
        ):
            at = pl.multiple_of(((x_at * 8 + y) * 2 + core_at) * 256, 256)
            out_ref[:, pl.ds(at, 256)] = ref[back]


def exchange(pieces, axes):
    return lax.all_to_all(pieces, axes, 0, 0)


def swap(array, axes):
    count = 2 if isinstance(axes, str) else 4
    return lax.ppermute(array, axes, [(at, count - 1 - at) for at in range(count)])


def shift(array, by):
    return lax.ppermute(array, "y", [(at, (at + by) % 8) for at in range(8)])


def per_device(
    inputs,
    key_output_gradient,
    frozen_key_weight,
    adapter_first_factor,
    adapter_second_factor,
    privacy_noise_first,
    privacy_noise_second,
):
    place = jnp.stack([lax.axis_index(axis).astype(jnp.int32) for axis in ("core", "xh", "xl", "y")])

    factor_t = jnp.broadcast_to(adapter_first_factor.T[None], (16, 64, 256))
    factor_t = exchange(factor_t, ("xh", "y"))

    up, down = [frozen_key_weight], [frozen_key_weight]
    for _ in range(4):
        up.append(shift(up[-1], 1))
    for _ in range(3):
        down.append(shift(down[-1], 7))
    blocks = up + down[:0:-1]

    keep, send, order = pl.pallas_call(
        first_partials_kernel,
        in_specs=[SMEM] + [VMEM] * 3,
        out_shape=(jax.ShapeDtypeStruct((8, 64, 512), BF16),) * 2 + (jax.ShapeDtypeStruct((8, 128), F32),),
        name="first_partials",
    )(place, inputs, key_output_gradient, adapter_second_factor)
    first = pl.pallas_call(
        pair_sum_kernel, out_shape=jax.ShapeDtypeStruct((8, 64, 512), BF16), name="pair_sum"
    )(keep, swap(send, "xl"))
    first = exchange(first, "z")

    gradients = [key_output_gradient] + [swap(key_output_gradient, axes) for axes in ("core", "xh", ("xh", "core"))]

    second = pl.pallas_call(
        second_partials_kernel,
        in_specs=[SMEM] + [VMEM] * 4 + [ANY],
        out_shape=jax.ShapeDtypeStruct((CTX, 8, 512), BF16),
        scratch_shapes=[pltpu.VMEM((640, 64), F32), pltpu.VMEM((88, 512), F32)],
        name="second_partials",
    )(place, inputs, key_output_gradient, factor_t, swap(factor_t, "core"), order)
    second = exchange(second, CTX_PARTS)

    products = pl.pallas_call(
        input_gradient_kernel,
        in_specs=[SMEM] + [VMEM] * 14,
        out_shape=[jax.ShapeDtypeStruct((8, 128, 256), BF16)] * 4,
        compiler_params=pltpu.CompilerParams(vmem_limit_bytes=40 << 20),
        name="input_gradient",
    )(place, *gradients, adapter_second_factor, factor_t, *blocks)
    products = [products[0]] + [
        swap(product, axes) for product, axes in zip(products[1:], ("core", "xh", ("xh", "core")))
    ]
    d_input = pl.pallas_call(
        interleave_kernel,
        in_specs=[SMEM] + [VMEM] * 4,
        out_shape=jax.ShapeDtypeStruct((128, 8192), BF16),
        name="interleave",
    )(place, *products)

    shares = pl.pallas_call(
        document_share_kernel,
        out_shape=jax.ShapeDtypeStruct((DOCS, 16, 128), BF16),
        name="document_share",
    )(first, second)
    shares = exchange(shares, DP_PARTS)

    squares = pl.pallas_call(
        squares_kernel,
        out_shape=jax.ShapeDtypeStruct((CTX, 8, 128), F32),
        name="squares",
    )(shares)
    squares = exchange(squares, CTX_PARTS)

    tiles = pl.pallas_call(
        clipped_sum_kernel,
        out_shape=jax.ShapeDtypeStruct((DOCS, 16, 128), F32),
        name="clipped_sum",
    )(shares, squares)
    tiles = exchange(tiles, DP_PARTS)

    grad_a, grad_b = pl.pallas_call(
        finish_kernel,
        in_specs=[VMEM] * 3 + [ANY],
        out_shape=(jax.ShapeDtypeStruct((64, 512), F32), jax.ShapeDtypeStruct((40, 64), F32)),
        scratch_shapes=[pltpu.VMEM((8, 512), F32)],
        name="finish",
    )(tiles, privacy_noise_first.T, privacy_noise_second.T, d_input)
    return (d_input, grad_a.T, grad_b.T)


def solution(mesh):
    parts = Mesh(mesh.devices.reshape(PART_SIZES), PARTS)
    return jax.shard_map(
        per_device,
        mesh=parts,
        in_specs=(
            P(PARTS, None),
            P(PARTS, None),
            P(DP_PARTS, None),
            P(DP_PARTS, None),
            P(),
            P(CTX_PARTS, None),
            P(None, CTX_PARTS),
        ),
        out_specs=(P(PARTS, None), P(CTX_PARTS, None), P(None, CTX_PARTS)),
        check_vma=False,
    )
```

time: 693 us -> 175 us (0.25)
  waiting for transfers between devices: 453 us -> 34.5 us
  blocking collectives: 198 us -> 16.1 us
  starting transfers between devices: 0.16 us -> 90.7 us
  Pallas kernels: 0 us -> 23.5 us
  between operations: 16.6 us -> 0.99 us
  matrix products: 14.7 us -> 0 us
  other arithmetic: 9.95 us -> 0.6 us
  local copies, waits for them, and re-layouts: 0.79 us -> 7.83 us
    psum x2 -> x0, waiting for transfers between devices: 252 us -> none  [the longest x1 136 us: per_device(): lax.psum(part_a.astype(jnp.bfloat16), 'ctx').astype(jnp.float32)]
    all_gather x2 -> x0, waiting for transfers between devices: 199 us -> none  [the longest x1 115 us: per_device(): w_piece = lax.all_gather(frozen_key_weight, 'dp', axis=0, tiled=True)]
    psum x2 -> x0, blocking collectives: 198 us -> none  [the longest x1 123 us: per_device(): sum_a, sum_b = lax.psum((factor * share_a, factor * share_b), 'dp')]
    ppermute x0 -> x15, starting transfers between devices: none -> 45.9 us  [the longest x8 25.3 us: swap(): lax.ppermute(array, axes, [(at, count - 1 - at) for at in range(count)])]
    all_to_all x0 -> x5, starting transfers between devices: none -> 44.7 us  [exchange(): return lax.all_to_all(pieces, axes, 0, 0)]
    ppermute x0 -> x15, waiting for transfers between devices: none -> 34.5 us  [the longest x8 28.4 us: swap(): lax.ppermute(array, axes, [(at, count - 1 - at) for at in range(count)])]
    pallas_call x0 -> x9, Pallas kernels: none -> 23.5 us  [the longest x1 4.2 us: per_device(): pl.pallas_call(input_gradient_kernel, in_specs=[SMEM] + [VMEM] * 14, out_...]
    all_to_all x0 -> x1, blocking collectives: none -> 16.1 us  [exchange(): return lax.all_to_all(pieces, axes, 0, 0)]
  transfers between devices with their start and end apart: 4 -> 20, of which waited for: 4 -> 4; matrix products, arithmetic and copies ran while one was open for 1% -> 0% of each run, Pallas kernels for 0% -> 12%
where the time goes in v1:
time: 175 us; the launch traced here: 174 us
  starting transfers between devices  90.7 us (52%)
  waiting for transfers between devices  34.5 us (20%)
  Pallas kernels  23.5 us (13%)
  blocking collectives  16.1 us (9%)
  local copies, waits for them, and re-layouts  7.83 us (4%)
    all_to_all x5, starting transfers between devices, exchange(): return lax.all_to_all(pieces, axes, 0, 0)  44.7 us
    ppermute x8, waiting for transfers between devices, swap(): lax.ppermute(array, axes, [(at, count - 1 - at) for at in range(count)])  28.4 us
    ppermute x8, starting transfers between devices, swap(): lax.ppermute(array, axes, [(at, count - 1 - at) for at in range(count)])  25.3 us
    ppermute x7, starting transfers between devices, shift(): return lax.ppermute(array, 'y', [(at, (at + by) % 8) for at in range(8)])  20.7 us
    all_to_all x1, blocking collectives, exchange(): return lax.all_to_all(pieces, axes, 0, 0)  16.1 us
    unnamed x32, local copies, waits for them, and re-layouts  6.23 us
    ppermute x7, waiting for transfers between devices, shift(): return lax.ppermute(array, 'y', [(at, (at + by) % 8) for at in range(8)])  6.04 us
    pallas_call x1, Pallas kernels, per_device(): pl.pallas_call(input_gradient_kernel, in_specs=[SMEM] + [VMEM] * 14, out_...  4.2 us
  transfers between devices with their start and end apart: 20, of which 4 were waited for; matrix products, arithmetic and copies ran while one was open for 0% of the time, Pallas kernels for 12%

profile of v1, /device:TPU:1, one launch (start us, length us, event | category | flops | bytes accessed | tf_op | source)
XLA Modules:
  0.0 174.2 jit_solution(7052867731405719757)
XLA Ops:
  0.6 1.6 broadcast_in_dim.2
  2.2 10.2 %all-to-all-start = ((bf16[16,64,256]{2,1,0:T(8,128)(2,1)}), bf16[16,64,256]{2,1,0:T(8,128)(2,1)S(1)}, u32[]{:S(2)}, u32[]{:S(2)}) async-start(bf16[16,64,256]{2,1,0:T(8,128)(2,1)} %broadcast_in_dim.2), calls=%async_computation | async-start | bytes 1048576 | tf_op jit(solution)/shard_map/all_to_all | solution.py:151
  12.5 0.6 pad_add_fusion.place_ref
  13.1 3.2 %first_partials.1 = (bf16[8,64,512]{2,1,0:T(8,128)(2,1)}, bf16[8,64,512]{2,1,0:T(8,128)(2,1)}, f32[8,128]{1,0:T(8,128)}) custom-call(s32[4]{0:T(128)} %pad_add_fusion.place_ref, bf16[128,8192]{1,0:T(8,128)(2,1)} %x_ref.3, bf16[128,640]{1,0:T(8,128)(2,1)} %g_ref.3, bf16[64,640]{1,0:T(8,128)(2,1)} %b_ref.1), custom_call_target="tpu_custom_call" | custom-call | tf_op jit(solution)/shard_map/first_partials/pallas_call | solution.py:184
  16.3 2.2 %collective-permute-start.13 = (bf16[8,64,512]{2,1,0:T(8,128)(2,1)}, bf16[8,64,512]{2,1,0:T(8,128)(2,1)S(1)}, u32[]{:S(2)}, u32[]{:S(2)}) collective-permute-start(bf16[8,64,512]{2,1,0:T(8,128)(2,1)} %get-tuple-element.17), channel_id=1, source_target_pairs={{0,1},{1,0},{2,3},{3,2},{4,5},{5,4},{6,7},{7,6},{8,9},{9,8},{10,11... | collective-permute-start | bytes 1572872 | tf_op jit(solution)/shard_map/ppermute | solution.py:156
  18.5 15.4 %collective-permute-done.13.b_ref = bf16[8,64,512]{2,1,0:T(8,128)(2,1)S(1)} collective-permute-done((bf16[8,64,512]{2,1,0:T(8,128)(2,1)}, bf16[8,64,512]{2,1,0:T(8,128)(2,1)S(1)}, u32[]{:S(2)}, u32[]{:S(2)}) %collective-permute-start.13) | collective-permute-done | bytes 524320 | tf_op jit(solution)/shard_map/ppermute | solution.py:156
  33.9 0.8 copy-done.13
  34.7 2.1 %pair_sum.1 = bf16[8,64,512]{2,1,0:T(8,128)(2,1)} custom-call(bf16[8,64,512]{2,1,0:T(8,128)(2,1)} %get-tuple-element.16.a_ref, bf16[8,64,512]{2,1,0:T(8,128)(2,1)} %copy-done.13), custom_call_target="tpu_custom_call" | custom-call | tf_op jit(solution)/shard_map/pair_sum/pallas_call | solution.py:190
  36.8 10.0 %all-to-all-start.1 = ((bf16[8,64,512]{2,1,0:T(8,128)(2,1)}), bf16[8,64,512]{2,1,0:T(8,128)(2,1)S(1)}, u32[]{:S(2)}, u32[]{:S(2)}) async-start(bf16[8,64,512]{2,1,0:T(8,128)(2,1)} %pair_sum.1), calls=%async_computation.1 | async-start | bytes 1048576 | tf_op jit(solution)/shard_map/all_to_all | solution.py:151
  46.9 2.6 %collective-permute-start.3 = (bf16[256,640]{1,0:T(8,128)(2,1)S(1)}, bf16[256,640]{1,0:T(8,128)(2,1)S(1)}, u32[]{:S(2)}, u32[]{:S(2)}) collective-permute-start(bf16[256,640]{1,0:T(8,128)(2,1)S(1)} %copy-done.4), channel_id=1, source_target_pairs={{0,32},{32,64},{64,96},{96,128},{128,160},{160,192},{192,224},{224... | collective-permute-start | bytes 983048 | tf_op jit(solution)/shard_map/ppermute | solution.py:160
  49.5 4.3 %collective-permute-start.14 = (bf16[16,64,256]{2,1,0:T(8,128)(2,1)S(1)}, bf16[16,64,256]{2,1,0:T(8,128)(2,1)S(1)}, u32[]{:S(2)}, u32[]{:S(2)}) collective-permute-start(bf16[16,64,256]{2,1,0:T(8,128)(2,1)S(1)} %all-to-all-done.refs_5_.own_ref), channel_id=1, source_target_pairs={{0,16},{16,0},{1,17},{17,1},{2,18},{18,2},{3,19},{19,3},{4,20},{20... | collective-permute-start | bytes 1572872 | tf_op jit(solution)/shard_map/ppermute | solution.py:156
  53.8 3.3 %collective-permute-start.7 = (bf16[256,640]{1,0:T(8,128)(2,1)S(1)}, bf16[256,640]{1,0:T(8,128)(2,1)S(1)}, u32[]{:S(2)}, u32[]{:S(2)}) collective-permute-start(bf16[256,640]{1,0:T(8,128)(2,1)S(1)} %copy-done.4), channel_id=1, source_target_pairs={{0,224},{32,0},{64,32},{96,64},{128,96},{160,128},{192,160},{224,1... | collective-permute-start | bytes 983048 | tf_op jit(solution)/shard_map/ppermute | solution.py:160
  57.1 0.9 collective-permute-done.3.refs_7_
  58.0 1.9 %collective-permute-start.4 = (bf16[256,640]{1,0:T(8,128)(2,1)S(1)}, bf16[256,640]{1,0:T(8,128)(2,1)S(1)}, u32[]{:S(2)}, u32[]{:S(2)}) collective-permute-start(bf16[256,640]{1,0:T(8,128)(2,1)S(1)} %collective-permute-done.3.refs_7_), channel_id=1, source_target_pairs={{0,32},{32,64},{64,96},{96,128},{128,160},{160,192},{192,224},{224... | collective-permute-start | bytes 983048 | tf_op jit(solution)/shard_map/ppermute | solution.py:160
  59.9 5.1 %collective-permute-done.7.refs_13_ = bf16[256,640]{1,0:T(8,128)(2,1)S(1)} collective-permute-done((bf16[256,640]{1,0:T(8,128)(2,1)S(1)}, bf16[256,640]{1,0:T(8,128)(2,1)S(1)}, u32[]{:S(2)}, u32[]{:S(2)}) %collective-permute-start.7) | collective-permute-done | bytes 327712 | tf_op jit(solution)/shard_map/ppermute | solution.py:160
  65.1 4.5 %collective-permute-start.8 = (bf16[256,640]{1,0:T(8,128)(2,1)S(1)}, bf16[256,640]{1,0:T(8,128)(2,1)S(1)}, u32[]{:S(2)}, u32[]{:S(2)}) collective-permute-start(bf16[256,640]{1,0:T(8,128)(2,1)S(1)} %collective-permute-done.7.refs_13_), channel_id=1, source_target_pairs={{0,224},{32,0},{64,32},{96,64},{128,96},{160,128},{192,160},{224,1... | collective-permute-start | bytes 983048 | tf_op jit(solution)/shard_map/ppermute | solution.py:160
  69.6 1.9 %collective-permute-start.5 = (bf16[256,640]{1,0:T(8,128)(2,1)S(1)}, bf16[256,640]{1,0:T(8,128)(2,1)S(1)}, u32[]{:S(2)}, u32[]{:S(2)}) collective-permute-start(bf16[256,640]{1,0:T(8,128)(2,1)S(1)} %collective-permute-done.4.refs_8_), channel_id=1, source_target_pairs={{0,32},{32,64},{64,96},{96,128},{128,160},{160,192},{192,224},{224... | collective-permute-start | bytes 983048 | tf_op jit(solution)/shard_map/ppermute | solution.py:160
  71.5 0.0 collective-permute-done.14.other_ref
  71.5 0.8 copy-done.14
  72.3 3.8 %second_partials.1 = bf16[16,8,512]{2,1,0:T(8,128)(2,1)} custom-call(s32[4]{0:T(128)} %pad_add_fusion.place_ref, bf16[128,8192]{1,0:T(8,128)(2,1)} %x_ref.3, bf16[128,640]{1,0:T(8,128)(2,1)} %g_ref.3, bf16[16,64,256]{2,1,0:T(8,128)(2,1)} %copy-done, bf16[16,64,256]{2,1,0:T(8,128)(2,1)} %copy-done.14, f32[8,128]{1,0:T(8,128)} %get-tuple-element.18.order_ref), custom_call_target="tpu_custom_call" | custom-call | tf_op jit(solution)/shard_map/second_partials/pallas_call | solution.py:197
  76.2 16.1 %all_to_all.30.second_ref = bf16[16,8,512]{2,1,0:T(8,128)(2,1)} all-to-all(bf16[16,8,512]{2,1,0:T(8,128)(2,1)} %second_partials.1), channel_id=1, replica_groups=mesh['xh'=2,'y'=8,'core'=2,'z'=8,'xl'=2] {'z','xl'}, dimensions={0} | all-to-all | bytes 262144 | tf_op jit(solution)/shard_map/all_to_all | solution.py:151
  92.3 1.9 %document_share.1 = bf16[32,16,128]{2,1,0:T(8,128)(2,1)} custom-call(bf16[8,64,512]{2,1,0:T(8,128)(2,1)} %copy-done.7, bf16[16,8,512]{2,1,0:T(8,128)(2,1)} %all_to_all.30.second_ref), custom_call_target="tpu_custom_call" | custom-call | tf_op jit(solution)/shard_map/document_share/pallas_call | solution.py:223
  94.2 12.4 %all-to-all-start.3 = ((bf16[32,16,128]{2,1,0:T(8,128)(2,1)}), bf16[32,16,128]{2,1,0:T(8,128)(2,1)S(1)}, u32[]{:S(2)}, u32[]{:S(2)}) async-start(bf16[32,16,128]{2,1,0:T(8,128)(2,1)} %document_share.1), calls=%async_computation.3 | async-start | bytes 262144 | tf_op jit(solution)/shard_map/all_to_all | solution.py:151
  106.6 4.5 %collective-permute-start.9 = (bf16[256,640]{1,0:T(8,128)(2,1)S(1)}, bf16[256,640]{1,0:T(8,128)(2,1)S(1)}, u32[]{:S(2)}, u32[]{:S(2)}) collective-permute-start(bf16[256,640]{1,0:T(8,128)(2,1)S(1)} %collective-permute-done.8.refs_12_), channel_id=1, source_target_pairs={{0,224},{32,0},{64,32},{96,64},{128,96},{160,128},{192,160},{224,1... | collective-permute-start | bytes 983048 | tf_op jit(solution)/shard_map/ppermute | solution.py:160
  111.1 0.0 collective-permute-done.5.refs_9_
  111.1 1.9 %collective-permute-start.6 = (bf16[256,640]{1,0:T(8,128)(2,1)S(1)}, bf16[256,640]{1,0:T(8,128)(2,1)S(1)}, u32[]{:S(2)}, u32[]{:S(2)}) collective-permute-start(bf16[256,640]{1,0:T(8,128)(2,1)S(1)} %collective-permute-done.5.refs_9_), channel_id=1, source_target_pairs={{0,32},{32,64},{64,96},{96,128},{128,160},{160,192},{192,224},{224... | collective-permute-start | bytes 983048 | tf_op jit(solution)/shard_map/ppermute | solution.py:160
  113.1 5.2 %collective-permute-start.2 = (bf16[128,640]{1,0:T(8,128)(2,1)S(1)}, bf16[128,640]{1,0:T(8,128)(2,1)S(1)}, u32[]{:S(2)}, u32[]{:S(2)}) collective-permute-start(bf16[128,640]{1,0:T(8,128)(2,1)S(1)} %copy-done.2), channel_id=1, source_target_pairs={{0,272},{16,256},{256,16},{272,0},{1,273},{17,257},{257,17},{273,1... | collective-permute-start | bytes 491528 | tf_op jit(solution)/shard_map/ppermute | solution.py:156
  118.3 2.1 %collective-permute-start.1 = (bf16[128,640]{1,0:T(8,128)(2,1)S(1)}, bf16[128,640]{1,0:T(8,128)(2,1)S(1)}, u32[]{:S(2)}, u32[]{:S(2)}) collective-permute-start(bf16[128,640]{1,0:T(8,128)(2,1)S(1)} %copy-done.2), channel_id=1, source_target_pairs={{0,256},{256,0},{1,257},{257,1},{2,258},{258,2},{3,259},{259,3},{4... | collective-permute-start | bytes 491528 | tf_op jit(solution)/shard_map/ppermute | solution.py:156
  120.4 2.1 %collective-permute-start = (bf16[128,640]{1,0:T(8,128)(2,1)S(1)}, bf16[128,640]{1,0:T(8,128)(2,1)S(1)}, u32[]{:S(2)}, u32[]{:S(2)}) collective-permute-start(bf16[128,640]{1,0:T(8,128)(2,1)S(1)} %copy-done.2), channel_id=1, source_target_pairs={{0,16},{16,0},{1,17},{17,1},{2,18},{18,2},{3,19},{19,3},{4,20},{20... | collective-permute-start | bytes 491528 | tf_op jit(solution)/shard_map/ppermute | solution.py:156
  122.5 0.0 copy-start.8
  122.5 0.6 copy-done.8
  123.2 1.6 squares.1
  124.8 3.5 %all-to-all-start.4 = ((f32[16,8,128]{2,1,0:T(8,128)}), f32[16,8,128]{2,1,0:T(8,128)S(1)}, u32[]{:S(2)}, u32[]{:S(2)}) async-start(f32[16,8,128]{2,1,0:T(8,128)} %squares.1), calls=%async_computation.4 | async-start | bytes 131072 | tf_op jit(solution)/shard_map/all_to_all | solution.py:151
  128.3 0.0 copy-start.1
  128.3 1.0 copy-done.1
  129.4 4.2 %input_gradient.1 = (bf16[8,128,256]{2,1,0:T(8,128)(2,1)S(1)}, bf16[8,128,256]{2,1,0:T(8,128)(2,1)}, bf16[8,128,256]{2,1,0:T(8,128)(2,1)}, bf16[8,128,256]{2,1,0:T(8,128)(2,1)}) custom-call(s32[4]{0:T(128)S(1)} %copy-done.6, bf16[128,640]{1,0:T(8,128)(2,1)S(1)} %copy-done.2, bf16[128,640]{1,0:T(8,128)(2,1)S(1)} %collective-permute-done.refs_1_, ...), custom_call_target="tpu_custom_call" | custom-call | tf_op jit(solution)/shard_map/input_gradient/pallas_call | solution.py:206
  133.6 0.8 copy-done.3
  134.4 2.2 %collective-permute-start.10 = (bf16[8,128,256]{2,1,0:T(8,128)(2,1)}, bf16[8,128,256]{2,1,0:T(8,128)(2,1)S(1)}, u32[]{:S(2)}, u32[]{:S(2)}) collective-permute-start(bf16[8,128,256]{2,1,0:T(8,128)(2,1)} %get-tuple-element.13), channel_id=1, source_target_pairs={{0,16},{16,0},{1,17},{17,1},{2,18},{18,2},{3,19},{19,3},{4,20},{20... | collective-permute-start | bytes 1572872 | tf_op jit(solution)/shard_map/ppermute | solution.py:156
  136.6 4.7 %collective-permute-start.11 = (bf16[8,128,256]{2,1,0:T(8,128)(2,1)}, bf16[8,128,256]{2,1,0:T(8,128)(2,1)S(1)}, u32[]{:S(2)}, u32[]{:S(2)}) collective-permute-start(bf16[8,128,256]{2,1,0:T(8,128)(2,1)} %get-tuple-element.14), channel_id=1, source_target_pairs={{0,256},{256,0},{1,257},{257,1},{2,258},{258,2},{3,259},{259,3},{4... | collective-permute-start | bytes 1572872 | tf_op jit(solution)/shard_map/ppermute | solution.py:156
  141.2 2.5 %collective-permute-start.12 = (bf16[8,128,256]{2,1,0:T(8,128)(2,1)}, bf16[8,128,256]{2,1,0:T(8,128)(2,1)S(1)}, u32[]{:S(2)}, u32[]{:S(2)}) collective-permute-start(bf16[8,128,256]{2,1,0:T(8,128)(2,1)} %get-tuple-element.15), channel_id=1, source_target_pairs={{0,272},{16,256},{256,16},{272,0},{1,273},{17,257},{257,17},{273,1... | collective-permute-start | bytes 1572872 | tf_op jit(solution)/shard_map/ppermute | solution.py:156
  143.8 0.6 copy-done.15
  144.4 1.8 %clipped_sum.1 = f32[32,16,128]{2,1,0:T(8,128)} custom-call(bf16[32,16,128]{2,1,0:T(8,128)(2,1)} %copy-done.8, f32[16,8,128]{2,1,0:T(8,128)} %copy-done.15), custom_call_target="tpu_custom_call" | custom-call | tf_op jit(solution)/shard_map/clipped_sum/pallas_call | solution.py:237
  146.1 8.6 %all-to-all-start.5 = ((f32[32,16,128]{2,1,0:T(8,128)}), f32[32,16,128]{2,1,0:T(8,128)S(1)}, u32[]{:S(2)}, u32[]{:S(2)}) async-start(f32[32,16,128]{2,1,0:T(8,128)} %clipped_sum.1), calls=%async_computation.5 | async-start | bytes 524288 | tf_op jit(solution)/shard_map/all_to_all | solution.py:151
  154.8 13.0 %collective-permute-done.12.refs_3_ = bf16[8,128,256]{2,1,0:T(8,128)(2,1)S(1)} collective-permute-done((bf16[8,128,256]{2,1,0:T(8,128)(2,1)}, bf16[8,128,256]{2,1,0:T(8,128)(2,1)S(1)}, u32[]{:S(2)}, u32[]{:S(2)}) %collective-permute-start.12) | collective-permute-done | bytes 524320 | tf_op jit(solution)/shard_map/ppermute | solution.py:156
  167.8 0.8 copy-done.12
  168.6 3.1 %interleave.1.order_ref = bf16[128,8192]{1,0:T(8,128)(2,1)} custom-call(s32[4]{0:T(128)} %pad_add_fusion.place_ref, bf16[8,128,256]{2,1,0:T(8,128)(2,1)} %copy-done.3, bf16[8,128,256]{2,1,0:T(8,128)(2,1)} %copy-done.10, bf16[8,128,256]{2,1,0:T(8,128)(2,1)} %copy-done.11, bf16[8,128,256]{2,1,0:T(8,128)(2,1)} %copy-done.12), custom_call_target="tpu_custom_call" | custom-call | tf_op jit(solution)/shard_map/interleave/pallas_call | solution.py:216
  171.7 0.7 copy-done.9
  172.4 1.8 %finish.1 = (f32[64,512]{1,0:T(8,128)}, f32[40,64]{1,0:T(8,128)}) custom-call(f32[32,16,128]{2,1,0:T(8,128)} %copy-done.9, f32[64,512]{1,0:T(8,128)} %bitcast.9, f32[40,64]{1,0:T(8,128)} %bitcast.11, bf16[128,8192]{1,0:T(8,128)(2,1)} %interleave.1.order_ref), custom_call_target="tpu_custom_call" | custom-call | tf_op jit(solution)/shard_map/finish/pallas_call | solution.py:244
  (36 shorter events, 0.1 us)
Async XLA Ops:
  2.2 34.6 %all-to-all-start = ((bf16[16,64,256]{2,1,0:T(8,128)(2,1)}), bf16[16,64,256]{2,1,0:T(8,128)(2,1)S(1)}, u32[]{:S(2)}, u32[]{:S(2)}) async-start(bf16[16,64,256]{2,1,0:T(8,128)(2,1)} %broadcast_in_dim.2), calls=%async_computation | async-start | bytes 1048576 | tf_op jit(solution)/shard_map/all_to_all | solution.py:151
  13.1 33.8 %copy-start.4 = (bf16[256,640]{1,0:T(8,128)(2,1)S(1)}, bf16[256,640]{1,0:T(8,128)(2,1)}, u32[]{:S(2)}) copy-start(bf16[256,640]{1,0:T(8,128)(2,1)} %refs_6_.1) | copy-start | bytes 983044
  16.3 17.6 %collective-permute-start.13 = (bf16[8,64,512]{2,1,0:T(8,128)(2,1)}, bf16[8,64,512]{2,1,0:T(8,128)(2,1)S(1)}, u32[]{:S(2)}, u32[]{:S(2)}) collective-permute-start(bf16[8,64,512]{2,1,0:T(8,128)(2,1)} %get-tuple-element.17), channel_id=1, source_target_pairs={{0,1},{1,0},{2,3},{3,2},{4,5},{5,4},{6,7},{7,6},{8,9},{9,8},{10,11... | collective-permute-start | bytes 1572872 | tf_op jit(solution)/shard_map/ppermute | solution.py:156
  33.9 0.8 copy-start.13
  36.8 35.5 %copy-start = (bf16[16,64,256]{2,1,0:T(8,128)(2,1)}, bf16[16,64,256]{2,1,0:T(8,128)(2,1)S(1)}, u32[]{:S(2)}) copy-start(bf16[16,64,256]{2,1,0:T(8,128)(2,1)S(1)} %all-to-all-done.refs_5_.own_ref) | copy-start | bytes 1572868
  36.8 39.3 %all-to-all-start.1 = ((bf16[8,64,512]{2,1,0:T(8,128)(2,1)}), bf16[8,64,512]{2,1,0:T(8,128)(2,1)S(1)}, u32[]{:S(2)}, u32[]{:S(2)}) async-start(bf16[8,64,512]{2,1,0:T(8,128)(2,1)} %pair_sum.1), calls=%async_computation.1 | async-start | bytes 1048576 | tf_op jit(solution)/shard_map/all_to_all | solution.py:151
  46.9 11.1 %collective-permute-start.3 = (bf16[256,640]{1,0:T(8,128)(2,1)S(1)}, bf16[256,640]{1,0:T(8,128)(2,1)S(1)}, u32[]{:S(2)}, u32[]{:S(2)}) collective-permute-start(bf16[256,640]{1,0:T(8,128)(2,1)S(1)} %copy-done.4), channel_id=1, source_target_pairs={{0,32},{32,64},{64,96},{96,128},{128,160},{160,192},{192,224},{224... | collective-permute-start | bytes 983048 | tf_op jit(solution)/shard_map/ppermute | solution.py:160
  49.5 22.0 %collective-permute-start.14 = (bf16[16,64,256]{2,1,0:T(8,128)(2,1)S(1)}, bf16[16,64,256]{2,1,0:T(8,128)(2,1)S(1)}, u32[]{:S(2)}, u32[]{:S(2)}) collective-permute-start(bf16[16,64,256]{2,1,0:T(8,128)(2,1)S(1)} %all-to-all-done.refs_5_.own_ref), channel_id=1, source_target_pairs={{0,16},{16,0},{1,17},{17,1},{2,18},{18,2},{3,19},{19,3},{4,20},{20... | collective-permute-start | bytes 1572872 | tf_op jit(solution)/shard_map/ppermute | solution.py:156
  53.8 11.2 %collective-permute-start.7 = (bf16[256,640]{1,0:T(8,128)(2,1)S(1)}, bf16[256,640]{1,0:T(8,128)(2,1)S(1)}, u32[]{:S(2)}, u32[]{:S(2)}) collective-permute-start(bf16[256,640]{1,0:T(8,128)(2,1)S(1)} %copy-done.4), channel_id=1, source_target_pairs={{0,224},{32,0},{64,32},{96,64},{128,96},{160,128},{192,160},{224,1... | collective-permute-start | bytes 983048 | tf_op jit(solution)/shard_map/ppermute | solution.py:160
  58.0 11.5 %collective-permute-start.4 = (bf16[256,640]{1,0:T(8,128)(2,1)S(1)}, bf16[256,640]{1,0:T(8,128)(2,1)S(1)}, u32[]{:S(2)}, u32[]{:S(2)}) collective-permute-start(bf16[256,640]{1,0:T(8,128)(2,1)S(1)} %collective-permute-done.3.refs_7_), channel_id=1, source_target_pairs={{0,32},{32,64},{64,96},{96,128},{128,160},{160,192},{192,224},{224... | collective-permute-start | bytes 983048 | tf_op jit(solution)/shard_map/ppermute | solution.py:160
  65.1 41.5 %collective-permute-start.8 = (bf16[256,640]{1,0:T(8,128)(2,1)S(1)}, bf16[256,640]{1,0:T(8,128)(2,1)S(1)}, u32[]{:S(2)}, u32[]{:S(2)}) collective-permute-start(bf16[256,640]{1,0:T(8,128)(2,1)S(1)} %collective-permute-done.7.refs_13_), channel_id=1, source_target_pairs={{0,224},{32,0},{64,32},{96,64},{128,96},{160,128},{192,160},{224,1... | collective-permute-start | bytes 983048 | tf_op jit(solution)/shard_map/ppermute | solution.py:160
  69.6 41.6 %collective-permute-start.5 = (bf16[256,640]{1,0:T(8,128)(2,1)S(1)}, bf16[256,640]{1,0:T(8,128)(2,1)S(1)}, u32[]{:S(2)}, u32[]{:S(2)}) collective-permute-start(bf16[256,640]{1,0:T(8,128)(2,1)S(1)} %collective-permute-done.4.refs_8_), channel_id=1, source_target_pairs={{0,32},{32,64},{64,96},{96,128},{128,160},{160,192},{192,224},{224... | collective-permute-start | bytes 983048 | tf_op jit(solution)/shard_map/ppermute | solution.py:160
  71.5 0.8 copy-start.14
  72.3 40.7 %copy-start.2 = (bf16[128,640]{1,0:T(8,128)(2,1)S(1)}, bf16[128,640]{1,0:T(8,128)(2,1)}, u32[]{:S(2)}) copy-start(bf16[128,640]{1,0:T(8,128)(2,1)} %g_ref.3) | copy-start | bytes 491524
  72.3 56.0 %copy-start.5 = (bf16[64,640]{1,0:T(8,128)(2,1)S(1)}, bf16[64,640]{1,0:T(8,128)(2,1)}, u32[]{:S(2)}) copy-start(bf16[64,640]{1,0:T(8,128)(2,1)} %b_ref.1) | copy-start | bytes 245764
  72.3 56.0 %copy-start.6 = (s32[4]{0:T(128)S(1)}, s32[4]{0:T(128)}, u32[]{:S(2)}) copy-start(s32[4]{0:T(128)} %pad_add_fusion.place_ref) | copy-start | bytes 52
  76.2 16.1 %copy-start.7 = (bf16[8,64,512]{2,1,0:T(8,128)(2,1)}, bf16[8,64,512]{2,1,0:T(8,128)(2,1)S(1)}, u32[]{:S(2)}) copy-start(bf16[8,64,512]{2,1,0:T(8,128)(2,1)S(1)} %all-to-all-done.1.first_ref) | copy-start | bytes 1572868
  94.2 28.3 %all-to-all-start.3 = ((bf16[32,16,128]{2,1,0:T(8,128)(2,1)}), bf16[32,16,128]{2,1,0:T(8,128)(2,1)S(1)}, u32[]{:S(2)}, u32[]{:S(2)}) async-start(bf16[32,16,128]{2,1,0:T(8,128)(2,1)} %document_share.1), calls=%async_computation.3 | async-start | bytes 262144 | tf_op jit(solution)/shard_map/all_to_all | solution.py:151
  106.6 21.7 %collective-permute-start.9 = (bf16[256,640]{1,0:T(8,128)(2,1)S(1)}, bf16[256,640]{1,0:T(8,128)(2,1)S(1)}, u32[]{:S(2)}, u32[]{:S(2)}) collective-permute-start(bf16[256,640]{1,0:T(8,128)(2,1)S(1)} %collective-permute-done.8.refs_12_), channel_id=1, source_target_pairs={{0,224},{32,0},{64,32},{96,64},{128,96},{160,128},{192,160},{224,1... | collective-permute-start | bytes 983048 | tf_op jit(solution)/shard_map/ppermute | solution.py:160
  111.1 17.2 %collective-permute-start.6 = (bf16[256,640]{1,0:T(8,128)(2,1)S(1)}, bf16[256,640]{1,0:T(8,128)(2,1)S(1)}, u32[]{:S(2)}, u32[]{:S(2)}) collective-permute-start(bf16[256,640]{1,0:T(8,128)(2,1)S(1)} %collective-permute-done.5.refs_9_), channel_id=1, source_target_pairs={{0,32},{32,64},{64,96},{96,128},{128,160},{160,192},{192,224},{224... | collective-permute-start | bytes 983048 | tf_op jit(solution)/shard_map/ppermute | solution.py:160
  113.1 15.2 %collective-permute-start.2 = (bf16[128,640]{1,0:T(8,128)(2,1)S(1)}, bf16[128,640]{1,0:T(8,128)(2,1)S(1)}, u32[]{:S(2)}, u32[]{:S(2)}) collective-permute-start(bf16[128,640]{1,0:T(8,128)(2,1)S(1)} %copy-done.2), channel_id=1, source_target_pairs={{0,272},{16,256},{256,16},{272,0},{1,273},{17,257},{257,17},{273,1... | collective-permute-start | bytes 491528 | tf_op jit(solution)/shard_map/ppermute | solution.py:156
  118.3 10.0 %collective-permute-start.1 = (bf16[128,640]{1,0:T(8,128)(2,1)S(1)}, bf16[128,640]{1,0:T(8,128)(2,1)S(1)}, u32[]{:S(2)}, u32[]{:S(2)}) collective-permute-start(bf16[128,640]{1,0:T(8,128)(2,1)S(1)} %copy-done.2), channel_id=1, source_target_pairs={{0,256},{256,0},{1,257},{257,1},{2,258},{258,2},{3,259},{259,3},{4... | collective-permute-start | bytes 491528 | tf_op jit(solution)/shard_map/ppermute | solution.py:156
  120.4 7.9 %collective-permute-start = (bf16[128,640]{1,0:T(8,128)(2,1)S(1)}, bf16[128,640]{1,0:T(8,128)(2,1)S(1)}, u32[]{:S(2)}, u32[]{:S(2)}) collective-permute-start(bf16[128,640]{1,0:T(8,128)(2,1)S(1)} %copy-done.2), channel_id=1, source_target_pairs={{0,16},{16,0},{1,17},{17,1},{2,18},{18,2},{3,19},{19,3},{4,20},{20... | collective-permute-start | bytes 491528 | tf_op jit(solution)/shard_map/ppermute | solution.py:156
  122.5 0.7 copy-start.8
  124.8 19.0 %all-to-all-start.4 = ((f32[16,8,128]{2,1,0:T(8,128)}), f32[16,8,128]{2,1,0:T(8,128)S(1)}, u32[]{:S(2)}, u32[]{:S(2)}) async-start(f32[16,8,128]{2,1,0:T(8,128)} %squares.1), calls=%async_computation.4 | async-start | bytes 131072 | tf_op jit(solution)/shard_map/all_to_all | solution.py:151
  128.3 1.0 copy-start.1
  133.6 0.8 copy-start.3
  134.4 20.4 %collective-permute-start.10 = (bf16[8,128,256]{2,1,0:T(8,128)(2,1)}, bf16[8,128,256]{2,1,0:T(8,128)(2,1)S(1)}, u32[]{:S(2)}, u32[]{:S(2)}) collective-permute-start(bf16[8,128,256]{2,1,0:T(8,128)(2,1)} %get-tuple-element.13), channel_id=1, source_target_pairs={{0,16},{16,0},{1,17},{17,1},{2,18},{18,2},{3,19},{19,3},{4,20},{20... | collective-permute-start | bytes 1572872 | tf_op jit(solution)/shard_map/ppermute | solution.py:156
  136.6 18.2 %collective-permute-start.11 = (bf16[8,128,256]{2,1,0:T(8,128)(2,1)}, bf16[8,128,256]{2,1,0:T(8,128)(2,1)S(1)}, u32[]{:S(2)}, u32[]{:S(2)}) collective-permute-start(bf16[8,128,256]{2,1,0:T(8,128)(2,1)} %get-tuple-element.14), channel_id=1, source_target_pairs={{0,256},{256,0},{1,257},{257,1},{2,258},{258,2},{3,259},{259,3},{4... | collective-permute-start | bytes 1572872 | tf_op jit(solution)/shard_map/ppermute | solution.py:156
  141.2 26.6 %collective-permute-start.12 = (bf16[8,128,256]{2,1,0:T(8,128)(2,1)}, bf16[8,128,256]{2,1,0:T(8,128)(2,1)S(1)}, u32[]{:S(2)}, u32[]{:S(2)}) collective-permute-start(bf16[8,128,256]{2,1,0:T(8,128)(2,1)} %get-tuple-element.15), channel_id=1, source_target_pairs={{0,272},{16,256},{256,16},{272,0},{1,273},{17,257},{257,17},{273,1... | collective-permute-start | bytes 1572872 | tf_op jit(solution)/shard_map/ppermute | solution.py:156
  143.7 0.6 copy-start.15
  146.1 25.6 %all-to-all-start.5 = ((f32[32,16,128]{2,1,0:T(8,128)}), f32[32,16,128]{2,1,0:T(8,128)S(1)}, u32[]{:S(2)}, u32[]{:S(2)}) async-start(f32[32,16,128]{2,1,0:T(8,128)} %clipped_sum.1), calls=%async_computation.5 | async-start | bytes 524288 | tf_op jit(solution)/shard_map/all_to_all | solution.py:151
  154.8 13.0 %copy-start.10 = (bf16[8,128,256]{2,1,0:T(8,128)(2,1)}, bf16[8,128,256]{2,1,0:T(8,128)(2,1)S(1)}, u32[]{:S(2)}) copy-start(bf16[8,128,256]{2,1,0:T(8,128)(2,1)S(1)} %collective-permute-done.10.refs_1_) | copy-start | bytes 1572868
  154.8 13.0 %copy-start.11 = (bf16[8,128,256]{2,1,0:T(8,128)(2,1)}, bf16[8,128,256]{2,1,0:T(8,128)(2,1)S(1)}, u32[]{:S(2)}) copy-start(bf16[8,128,256]{2,1,0:T(8,128)(2,1)S(1)} %collective-permute-done.11.refs_2_) | copy-start | bytes 1572868
  167.8 0.8 copy-start.12
  171.7 0.7 copy-start.9

commit v2 on v1

v2 whole, which is shorter than its diff:
```python
import jax
import jax.numpy as jnp
from jax import lax
from jax.experimental import pallas as pl
from jax.experimental.pallas import tpu as pltpu
from jax.sharding import Mesh, PartitionSpec as P

ADAPTER_SCALE = 2.0
NOISE = 0.005
DOCS = 32
CTX = 16
BF16 = jnp.bfloat16
F32 = jnp.float32

PARTS = ("xh", "y", "core", "z", "xl")
PART_SIZES = (2, 8, 2, 8, 2)
DP_PARTS = ("xh", "y", "core")
CTX_PARTS = ("z", "xl")

NT = (((1,), (1,)), ((), ()))
NN = (((1,), (0,)), ((), ()))

VMEM_LIMIT = pltpu.CompilerParams(vmem_limit_bytes=24 << 20)
SMEM = pl.BlockSpec(memory_space=pltpu.SMEM)
VMEM = pl.BlockSpec(memory_space=pltpu.VMEM)
ANY = pl.BlockSpec(memory_space=pl.ANY)


def in_vmem(*arrays):
    return [pltpu.with_memory_space_constraint(array, pltpu.VMEM) for array in arrays]


def in_hbm(*arrays):
    return [pltpu.with_memory_space_constraint(array, pltpu.HBM) for array in arrays]


def dot(a, b, dims):
    return lax.dot_general(a, b, dims, preferred_element_type=F32)


def three_terms(value):
    high = value.astype(BF16).astype(F32)
    middle = (value - high).astype(BF16).astype(F32)
    return high, middle, value - high - middle


def copies_kernel(in_ref, out_ref):
    for at in range(16):
        out_ref[at] = in_ref[...]


def partials_kernel(place_ref, x_ref, g_ref, b_ref, own_ref, other_ref, *refs):
    msg_ref, gbt_ref, z_ref = refs[-3:]
    core = place_ref[0]
    g = g_ref[...]
    u_t = (ADAPTER_SCALE * dot(b_ref[...], g, NT)).astype(BF16)
    h_t = jnp.zeros((64, 128), F32)
    for block in range(16):
        own_at = pl.multiple_of((2 * block + core) * 256, 256)
        other_at = pl.multiple_of((2 * block + 1 - core) * 256, 256)
        h_t += dot(own_ref[block], x_ref[:, pl.ds(own_at, 256)], NT)
        h_t += dot(other_ref[block], x_ref[:, pl.ds(other_at, 256)], NT)
    for j in range(CTX):
        msg_ref[j, 0:64, :] = dot(u_t, x_ref[:, 512 * j : 512 * j + 512], NN).astype(BF16)
    gbt_ref[...] = ADAPTER_SCALE * dot(g.T, h_t.astype(BF16), NT)
    for q in range(8):
        z_ref[0:80, 64 * q : 64 * q + 64] = gbt_ref[pl.ds(q, 80, stride=8), :]
    z_ref[80:88, :] = jnp.zeros((8, 512), F32)
    keep = lax.broadcasted_iota(jnp.int32, (8, 512), 0) < 5
    for j in range(CTX):
        msg_ref[j, 64:72, :] = jnp.where(keep, z_ref[5 * j : 5 * j + 8, :], 0.0).astype(BF16)


def wait_kernel(*refs):
    pass


def document_share_kernel(parts_ref, up_ref, down_ref, share_ref, square_ref):
    total = parts_ref[0].astype(F32)
    for j in range(1, CTX):
        total += parts_ref[j].astype(F32)
    share_ref[...] = total
    square = jnp.sum(total * total, axis=0, keepdims=True)
    square = jnp.broadcast_to(jnp.sum(square, axis=1, keepdims=True), (8, 128))
    for j in range(CTX):
        square_ref[j] = square


def document_messages_kernel(share_ref, squares_ref, _, out_ref):
    square = squares_ref[0]
    for j in range(1, CTX):
        square += squares_ref[j]
    high, middle, low = three_terms(jnp.sqrt(square))
    row = lax.broadcasted_iota(jnp.int32, (8, 128), 0)
    norm = jnp.where(row == 1, high, jnp.where(row == 2, middle, jnp.where(row == 3, low, 0.0)))
    for k in range(DOCS):
        a, lane = k // 4, 128 * (k % 4)
        tail = jnp.where(row == 0, share_ref[64 + a : 65 + a, lane : lane + 128], norm)
        tile = share_ref[8 * a : 8 * a + 8, lane : lane + 128]
        out_ref[k] = jnp.concatenate([tile, tail], axis=0).astype(BF16)


def clipped_sum_kernel(messages_ref, out_ref):
    norms = messages_ref[:, 9, :].astype(F32) + messages_ref[:, 10, :].astype(F32) + messages_ref[:, 11, :].astype(F32)
    bound = jnp.sum(norms, axis=0, keepdims=True) / DOCS
    factor = bound / jnp.maximum(norms, bound)
    total = factor[0:1] * messages_ref[0].astype(F32)
    for k in range(1, DOCS):
        total += factor[k : k + 1] * messages_ref[k].astype(F32)
    high, middle, low = three_terms(bound)
    row = lax.broadcasted_iota(jnp.int32, (16, 128), 0)
    total = jnp.where(row == 9, high, jnp.where(row == 10, middle, jnp.where(row == 11, low, total))).astype(BF16)
    for k in range(DOCS):
        out_ref[k] = total


def finish_kernel(tiles_ref, noise_a_ref, noise_b_ref, _, grad_a_ref, grad_b_ref, z_ref):
    own = tiles_ref[0].astype(F32)
    noise = NOISE * (own[9:10, 0:1] + own[10:11, 0:1] + own[11:12, 0:1])
    for k in range(DOCS):
        a, lane = 8 * (k // 4), 128 * (k % 4)
        tile = tiles_ref[k].astype(F32)
        grad_a_ref[a : a + 8, lane : lane + 128] = (
            tile[0:8] + noise * noise_a_ref[a : a + 8, lane : lane + 128]
        ) / DOCS
        z_ref[k // 4 : k // 4 + 1, lane : lane + 128] = tile[8:9]
    for q in range(8):
        at = pl.ds(q, 5, stride=8)
        grad_b_ref[at, :] = (z_ref[0:5, 64 * q : 64 * q + 64] + noise * noise_b_ref[at, :]) / DOCS


def own_rows_kernel(place_ref, own_ref, other_ref, out_ref):
    out_ref[place_ref[1]] = own_ref[...]
    out_ref[1 - place_ref[1]] = other_ref[...]


def input_gradient_kernel(place_ref, *refs):
    g_refs, (b_ref, at_ref), w_refs, out_refs = refs[0:4], refs[4:6], refs[6:14], refs[14:18]
    g = jnp.concatenate([ref[...] for ref in g_refs], axis=0)
    u = (ADAPTER_SCALE * dot(g, b_ref[...], NT)).astype(BF16)
    half = pl.ds(pl.multiple_of(place_ref[2] * 128, 128), 128)
    for back in range(8):
        y = (place_ref[3] + 8 - back) % 8
        for xh in range(2):
            out = (dot(g, w_refs[back][xh], NT) + dot(u, at_ref[xh * 8 + y, :, half], NN)).astype(BF16)
            for at, ref in enumerate(out_refs):
                ref[back, :, 128 * xh : 128 * xh + 128] = out[128 * at : 128 * at + 128]


def interleave_kernel(place_ref, *refs):
    own_ref, core_ref, xl_ref, both_ref, out_ref = refs
    core, xl = place_ref[0], place_ref[2]
    for back in range(8):
        y = (place_ref[3] + 8 - back) % 8
        for ref, xl_at, core_at in (
            (own_ref, xl, core),
            (core_ref, xl, 1 - core),
            (xl_ref, 1 - xl, core),
            (both_ref, 1 - xl, 1 - core),
        ):
            for xh in range(2):
                at = pl.multiple_of((((xh * 8 + y) * 2 + core_at) * 2 + xl_at) * 128, 128)
                out_ref[:, pl.ds(at, 128)] = ref[back, :, 128 * xh : 128 * xh + 128]


def exchange(pieces, axes):
    return lax.all_to_all(pieces, axes, 0, 0)


def swap(array, axes):
    count = 2 if isinstance(axes, str) else 4
    return lax.ppermute(array, axes, [(at, count - 1 - at) for at in range(count)])


def shift(array, axis, by):
    return lax.ppermute(array, axis, [(at, (at + by) % 8) for at in range(8)])


def per_device(
    inputs,
    key_output_gradient,
    frozen_key_weight,
    adapter_first_factor,
    adapter_second_factor,
    privacy_noise_first,
    privacy_noise_second,
):
    place = jnp.stack([lax.axis_index(axis).astype(jnp.int32) for axis in ("core", "xh", "xl", "y", "z")])

    factor_t = pl.pallas_call(
        copies_kernel,
        in_specs=[VMEM],
        out_shape=pltpu.VMEM((16, 64, 256), BF16),
        compiler_params=VMEM_LIMIT,
        name="copies",
    )(adapter_first_factor.T)
    factor_t = exchange(factor_t, ("xh", "y"))

    gradients = [swap(key_output_gradient, axes) for axes in ("core", "xl", ("core", "xl"))]
    half = lax.dynamic_slice_in_dim(frozen_key_weight, place[2] * 128, 128, 0)
    near = pl.pallas_call(
        own_rows_kernel,
        in_specs=[SMEM] + [VMEM] * 2,
        out_shape=pltpu.VMEM((2, 128, 640), BF16),
        compiler_params=VMEM_LIMIT,
        name="own_rows",
    )(place, *in_vmem(half, swap(half, "xh")))
    factor_t = pl.pallas_call(
        wait_kernel,
        in_specs=[VMEM] * 5,
        out_shape=pltpu.VMEM(factor_t.shape, BF16),
        input_output_aliases={0: 0},
        compiler_params=VMEM_LIMIT,
        name="wait",
    )(*in_vmem(factor_t, near, *gradients))
    parts = pl.pallas_call(
        partials_kernel,
        in_specs=[SMEM] + [VMEM] * 5,
        out_shape=pltpu.VMEM((CTX, 72, 512), BF16),
        scratch_shapes=[pltpu.VMEM((640, 64), F32), pltpu.VMEM((88, 512), F32)],
        compiler_params=VMEM_LIMIT,
        name="partials",
    )(
        place,
        *in_hbm(inputs, key_output_gradient, adapter_second_factor),
        *in_vmem(factor_t, swap(factor_t, "core")),
    )
    parts = exchange(parts, CTX_PARTS)

    up1, down1 = in_hbm(shift(near, "y", 1), shift(near, "y", 7))
    up2, down2 = in_hbm(shift(up1, "y", 1), shift(down1, "y", 7))
    up3, down3 = in_hbm(shift(up2, "y", 1), shift(down2, "y", 7))
    (up4,) = in_hbm(shift(up3, "y", 1))
    blocks = [near, up1, up2, up3, up4, down3, down2, down1]
    share, squares = pl.pallas_call(
        document_share_kernel,
        in_specs=[VMEM, ANY, ANY],
        out_shape=(pltpu.VMEM((72, 512), F32), pltpu.VMEM((CTX, 8, 128), F32)),
        compiler_params=VMEM_LIMIT,
        name="document_share",
    )(*in_vmem(parts), *in_hbm(up3, down3))
    squares = exchange(squares, CTX_PARTS)

    products = pl.pallas_call(
        input_gradient_kernel,
        in_specs=[SMEM] + [VMEM] * 14,
        out_shape=[jax.ShapeDtypeStruct((8, 128, 256), BF16)] * 4,
        compiler_params=VMEM_LIMIT,
        name="input_gradient",
    )(place, key_output_gradient, *in_vmem(*gradients), adapter_second_factor, *in_vmem(factor_t, near), *in_hbm(*blocks[1:]))
    own = products[0]
    products = [own] + [
        swap(product, axes) for product, axes in zip(products[1:], ("core", "xl", ("core", "xl")))
    ]
    d_input = pl.pallas_call(
        interleave_kernel,
        in_specs=[SMEM] + [VMEM] * 4,
        out_shape=pltpu.HBM((128, 8192), BF16),
        compiler_params=VMEM_LIMIT,
        name="interleave",
    )(place, products[0], *in_vmem(*products[1:]))

    messages = pl.pallas_call(
        document_messages_kernel,
        in_specs=[VMEM, VMEM, ANY],
        out_shape=pltpu.VMEM((DOCS, 16, 128), BF16),
        compiler_params=VMEM_LIMIT,
        name="document_messages",
    )(*in_vmem(share, squares), own)
    messages = exchange(messages, DP_PARTS)

    tiles = pl.pallas_call(
        clipped_sum_kernel,
        in_specs=[VMEM],
        out_shape=pltpu.VMEM((DOCS, 16, 128), BF16),
        compiler_params=VMEM_LIMIT,
        name="clipped_sum",
    )(*in_vmem(messages))
    tiles = exchange(tiles, DP_PARTS)

    grad_a, grad_b = pl.pallas_call(
        finish_kernel,
        in_specs=[VMEM] * 3 + [ANY],
        out_shape=(jax.ShapeDtypeStruct((64, 512), F32), jax.ShapeDtypeStruct((40, 64), F32)),
        scratch_shapes=[pltpu.VMEM((8, 512), F32)],
        compiler_params=VMEM_LIMIT,
        name="finish",
    )(*in_vmem(tiles, privacy_noise_first.T, privacy_noise_second.T), *in_hbm(d_input))
    return (d_input, grad_a.T, grad_b.T)


def solution(mesh):
    parts = Mesh(mesh.devices.reshape(PART_SIZES), PARTS)
    return jax.shard_map(
        per_device,
        mesh=parts,
        in_specs=(
            P(PARTS, None),
            P(PARTS, None),
            P(DP_PARTS, None),
            P(DP_PARTS, None),
            P(),
            P(CTX_PARTS, None),
            P(None, CTX_PARTS),
        ),
        out_specs=(P(PARTS, None), P(CTX_PARTS, None), P(None, CTX_PARTS)),
        check_vma=False,
    )
```

time: 175 us -> 158 us (0.903)
  blocking collectives: 16.1 us -> 23.5 us
  local copies, waits for them, and re-layouts: 7.83 us -> 0.95 us
  Pallas kernels: 23.5 us -> 17.1 us
  waiting for transfers between devices: 34.5 us -> 28.8 us
  starting transfers between devices: 90.7 us -> 86 us
    ppermute x8, waiting for transfers between devices: 28.4 us -> 7.94 us  [swap(): lax.ppermute(array, axes, [(at, count - 1 - at) for at in range(count)])]
    all_to_all x5 -> x4, waiting for transfers between devices: 0.01 us -> 8.04 us  [exchange(): return lax.all_to_all(pieces, axes, 0, 0)]
    all_to_all x5 -> x4, starting transfers between devices: 44.7 us -> 36.8 us  [exchange(): return lax.all_to_all(pieces, axes, 0, 0)]
    all_to_all x1, blocking collectives: 16.1 us -> 23.5 us  [exchange(): return lax.all_to_all(pieces, axes, 0, 0)]
    pallas_call x6 -> x7, Pallas kernels: 14.5 us -> 7.42 us  [the longest x1 4.3 us: per_device(): pl.pallas_call(partials_kernel, in_specs=[SMEM] + [VMEM] * 5, out_shape=p...]
    ppermute x7, waiting for transfers between devices: 6.04 us -> 12.8 us  [shift(): return lax.ppermute(array, axis, [(at, (at + by) % 8) for at in range(8)])]
    unnamed x32 -> x20, local copies, waits for them, and re-layouts: 6.23 us -> 0.84 us
    ppermute x8, starting transfers between devices: 25.3 us -> 27.9 us  [swap(): lax.ppermute(array, axes, [(at, count - 1 - at) for at in range(count)])]
  transfers between devices with their start and end apart: 20 -> 19, of which waited for: 4 -> 7; matrix products, arithmetic and copies ran while one was open for 0% -> 0% of each run, Pallas kernels for 12% -> 7%
where the time goes in v2:
time: 158 us; the launch traced here: 157 us
  starting transfers between devices  86 us (54%)
  waiting for transfers between devices  28.8 us (18%)
  blocking collectives  23.5 us (15%)
  Pallas kernels  17.1 us (11%)
    all_to_all x4, starting transfers between devices, exchange(): return lax.all_to_all(pieces, axes, 0, 0)  36.8 us
    ppermute x8, starting transfers between devices, swap(): lax.ppermute(array, axes, [(at, count - 1 - at) for at in range(count)])  27.9 us
    all_to_all x1, blocking collectives, exchange(): return lax.all_to_all(pieces, axes, 0, 0)  23.5 us
    ppermute x7, starting transfers between devices, shift(): return lax.ppermute(array, axis, [(at, (at + by) % 8) for at in range(8)])  21.4 us
    ppermute x7, waiting for transfers between devices, shift(): return lax.ppermute(array, axis, [(at, (at + by) % 8) for at in range(8)])  12.8 us
    all_to_all x4, waiting for transfers between devices, exchange(): return lax.all_to_all(pieces, axes, 0, 0)  8.04 us
    ppermute x8, waiting for transfers between devices, swap(): lax.ppermute(array, axes, [(at, count - 1 - at) for at in range(count)])  7.94 us
    pallas_call x1, Pallas kernels, per_device(): pl.pallas_call(input_gradient_kernel, in_specs=[SMEM] + [VMEM] * 14, out_...  6.45 us
  transfers between devices with their start and end apart: 19, of which 7 were waited for; matrix products, arithmetic and copies ran while one was open for 0% of the time, Pallas kernels for 7%

profile of v2, /device:TPU:1, one launch (start us, length us, event | category | flops | bytes accessed | tf_op | source)
XLA Modules:
  0.0 157.4 jit_solution(17573712492887239344)
XLA Ops:
  0.6 0.0 copy-start
  0.7 0.8 copy-done.4
  1.5 0.8 copies.1
  2.3 10.2 %all-to-all-start = ((bf16[16,64,256]{2,1,0:T(8,128)(2,1)}), bf16[16,64,256]{2,1,0:T(8,128)(2,1)S(1)}, u32[]{:S(2)}, u32[]{:S(2)}) async-start(bf16[16,64,256]{2,1,0:T(8,128)(2,1)} %copies.1), calls=%async_computation | async-start | bytes 1048576 | tf_op jit(solution)/shard_map/all_to_all | solution.py:167
  12.5 4.8 %collective-permute-start.3 = (bf16[128,640]{1,0:T(8,128)(2,1)S(1)}, bf16[128,640]{1,0:T(8,128)(2,1)S(1)}, u32[]{:S(2)}, u32[]{:S(2)}) collective-permute-start(bf16[128,640]{1,0:T(8,128)(2,1)S(1)} %constant_dynamic-slice_fusion.own_ref), channel_id=1, source_target_pairs={{0,256},{256,0},{1,257},{257,1},{2,258},{258,2},{3,259},{259,3},{4... | collective-permute-start | bytes 491528 | tf_op jit(solution)/shard_map/ppermute | solution.py:172
  17.3 3.6 %collective-permute-start.2 = (bf16[128,640]{1,0:T(8,128)(2,1)}, bf16[128,640]{1,0:T(8,128)(2,1)S(1)}, u32[]{:S(2)}, u32[]{:S(2)}) collective-permute-start(bf16[128,640]{1,0:T(8,128)(2,1)} %g_ref.1), channel_id=1, source_target_pairs={{0,17},{1,16},{16,1},{17,0},{2,19},{3,18},{18,3},{19,2},{4,21},{5,... | collective-permute-start | bytes 491528 | tf_op jit(solution)/shard_map/ppermute | solution.py:172
  21.0 3.1 %collective-permute-start.1 = (bf16[128,640]{1,0:T(8,128)(2,1)}, bf16[128,640]{1,0:T(8,128)(2,1)S(1)}, u32[]{:S(2)}, u32[]{:S(2)}) collective-permute-start(bf16[128,640]{1,0:T(8,128)(2,1)} %g_ref.1), channel_id=1, source_target_pairs={{0,1},{1,0},{2,3},{3,2},{4,5},{5,4},{6,7},{7,6},{8,9},{9,8},{10,11... | collective-permute-start | bytes 491528 | tf_op jit(solution)/shard_map/ppermute | solution.py:172
  24.0 1.9 %collective-permute-start = (bf16[128,640]{1,0:T(8,128)(2,1)}, bf16[128,640]{1,0:T(8,128)(2,1)S(1)}, u32[]{:S(2)}, u32[]{:S(2)}) collective-permute-start(bf16[128,640]{1,0:T(8,128)(2,1)} %g_ref.1), channel_id=1, source_target_pairs={{0,16},{16,0},{1,17},{17,1},{2,18},{18,2},{3,19},{19,3},{4,20},{20... | collective-permute-start | bytes 491528 | tf_op jit(solution)/shard_map/ppermute | solution.py:172
  26.0 0.1 stack.23.place_ref
  26.1 0.6 own_rows.1.refs_1_.refs_6_
  26.6 3.6 %collective-permute-done.2.refs_4_.refs_3_ = bf16[128,640]{1,0:T(8,128)(2,1)S(1)} collective-permute-done((bf16[128,640]{1,0:T(8,128)(2,1)}, bf16[128,640]{1,0:T(8,128)(2,1)S(1)}, u32[]{:S(2)}, u32[]{:S(2)}) %collective-permute-start.2) | collective-permute-done | bytes 163872 | tf_op jit(solution)/shard_map/ppermute | solution.py:172
  30.3 2.8 %collective-permute-done.1.refs_3_.refs_2_ = bf16[128,640]{1,0:T(8,128)(2,1)S(1)} collective-permute-done((bf16[128,640]{1,0:T(8,128)(2,1)}, bf16[128,640]{1,0:T(8,128)(2,1)S(1)}, u32[]{:S(2)}, u32[]{:S(2)}) %collective-permute-start.1) | collective-permute-done | bytes 163872 | tf_op jit(solution)/shard_map/ppermute | solution.py:172
  33.0 0.0 collective-permute-done.refs_2_.refs_1_
  33.0 0.0 all-to-all-done.refs_0_
  33.1 2.8 %collective-permute-start.14 = (bf16[16,64,256]{2,1,0:T(8,128)(2,1)S(1)}, bf16[16,64,256]{2,1,0:T(8,128)(2,1)S(1)}, u32[]{:S(2)}, u32[]{:S(2)}) collective-permute-start(bf16[16,64,256]{2,1,0:T(8,128)(2,1)S(1)} %wait.1.refs_5_.own_ref), channel_id=1, source_target_pairs={{0,16},{16,0},{1,17},{17,1},{2,18},{18,2},{3,19},{19,3},{4,20},{20... | collective-permute-start | bytes 1572872 | tf_op jit(solution)/shard_map/ppermute | solution.py:172
  35.8 1.5 collective-permute-done.14.other_ref
  37.4 4.3 %partials.1 = bf16[16,72,512]{2,1,0:T(8,128)(2,1)} custom-call(s32[5]{0:T(128)S(1)} %stack.23.place_ref, bf16[128,8192]{1,0:T(8,128)(2,1)} %x_ref.1, bf16[128,640]{1,0:T(8,128)(2,1)} %g_ref.1, bf16[64,640]{1,0:T(8,128)(2,1)} %b_ref.1, bf16[16,64,256]{2,1,0:T(8,128)(2,1)S(1)} %wait.1.refs_5_.own_ref, bf16[16,64,256]{2,1,0:T(8,128)(2,1)S(1)} %collective-permute-done.14.other_ref), custom_call_target="tpu_custom_call" | custom-call | tf_op jit(solution)/shard_map/partials/pallas_call | solution.py:216
  41.7 11.1 %all-to-all-start.1 = ((bf16[16,72,512]{2,1,0:T(8,128)(2,1)}), bf16[16,72,512]{2,1,0:T(8,128)(2,1)S(1)}, u32[]{:S(2)}, u32[]{:S(2)}) async-start(bf16[16,72,512]{2,1,0:T(8,128)(2,1)} %partials.1), calls=%async_computation.1 | async-start | bytes 2359296 | tf_op jit(solution)/shard_map/all_to_all | solution.py:167
  52.8 2.9 %collective-permute-start.4 = (bf16[2,128,640]{2,1,0:T(8,128)(2,1)S(1)}, bf16[2,128,640]{2,1,0:T(8,128)(2,1)S(1)}, u32[]{:S(2)}, u32[]{:S(2)}) collective-permute-start(bf16[2,128,640]{2,1,0:T(8,128)(2,1)S(1)} %own_rows.1.refs_1_.refs_6_), channel_id=1, source_target_pairs={{0,32},{32,64},{64,96},{96,128},{128,160},{160,192},{192,224},{224... | collective-permute-start | bytes 983048 | tf_op jit(solution)/shard_map/ppermute | solution.py:176
  55.8 3.5 %collective-permute-start.8 = (bf16[2,128,640]{2,1,0:T(8,128)(2,1)S(1)}, bf16[2,128,640]{2,1,0:T(8,128)(2,1)S(1)}, u32[]{:S(2)}, u32[]{:S(2)}) collective-permute-start(bf16[2,128,640]{2,1,0:T(8,128)(2,1)S(1)} %own_rows.1.refs_1_.refs_6_), channel_id=1, source_target_pairs={{0,224},{32,0},{64,32},{96,64},{128,96},{160,128},{192,160},{224,1... | collective-permute-start | bytes 983048 | tf_op jit(solution)/shard_map/ppermute | solution.py:176
  59.3 5.2 %collective-permute-done.4.refs_7_ = bf16[2,128,640]{2,1,0:T(8,128)(2,1)S(1)} collective-permute-done((bf16[2,128,640]{2,1,0:T(8,128)(2,1)S(1)}, bf16[2,128,640]{2,1,0:T(8,128)(2,1)S(1)}, u32[]{:S(2)}, u32[]{:S(2)}) %collective-permute-start.4) | collective-permute-done | bytes 327712 | tf_op jit(solution)/shard_map/ppermute | solution.py:176
  64.5 1.9 %collective-permute-start.5 = (bf16[2,128,640]{2,1,0:T(8,128)(2,1)S(1)}, bf16[2,128,640]{2,1,0:T(8,128)(2,1)S(1)}, u32[]{:S(2)}, u32[]{:S(2)}) collective-permute-start(bf16[2,128,640]{2,1,0:T(8,128)(2,1)S(1)} %collective-permute-done.4.refs_7_), channel_id=1, source_target_pairs={{0,32},{32,64},{64,96},{96,128},{128,160},{160,192},{192,224},{224... | collective-permute-start | bytes 983048 | tf_op jit(solution)/shard_map/ppermute | solution.py:176
  66.4 0.0 collective-permute-done.8.refs_13_
  66.4 4.6 %collective-permute-start.9 = (bf16[2,128,640]{2,1,0:T(8,128)(2,1)S(1)}, bf16[2,128,640]{2,1,0:T(8,128)(2,1)S(1)}, u32[]{:S(2)}, u32[]{:S(2)}) collective-permute-start(bf16[2,128,640]{2,1,0:T(8,128)(2,1)S(1)} %collective-permute-done.8.refs_13_), channel_id=1, source_target_pairs={{0,224},{32,0},{64,32},{96,64},{128,96},{160,128},{192,160},{224,1... | collective-permute-start | bytes 983048 | tf_op jit(solution)/shard_map/ppermute | solution.py:176
  71.0 4.2 %collective-permute-done.5.refs_8_ = bf16[2,128,640]{2,1,0:T(8,128)(2,1)S(1)} collective-permute-done((bf16[2,128,640]{2,1,0:T(8,128)(2,1)S(1)}, bf16[2,128,640]{2,1,0:T(8,128)(2,1)S(1)}, u32[]{:S(2)}, u32[]{:S(2)}) %collective-permute-start.5) | collective-permute-done | bytes 327712 | tf_op jit(solution)/shard_map/ppermute | solution.py:176
  75.3 1.9 %collective-permute-start.6 = (bf16[2,128,640]{2,1,0:T(8,128)(2,1)S(1)}, bf16[2,128,640]{2,1,0:T(8,128)(2,1)}, u32[]{:S(2)}, u32[]{:S(2)}) collective-permute-start(bf16[2,128,640]{2,1,0:T(8,128)(2,1)S(1)} %collective-permute-done.5.refs_8_), channel_id=1, source_target_pairs={{0,32},{32,64},{64,96},{96,128},{128,160},{160,192},{192,224},{224... | collective-permute-start | bytes 983048 | tf_op jit(solution)/shard_map/ppermute | solution.py:176
  77.2 0.0 collective-permute-done.9.refs_12_
  77.2 4.6 %collective-permute-start.10 = (bf16[2,128,640]{2,1,0:T(8,128)(2,1)S(1)}, bf16[2,128,640]{2,1,0:T(8,128)(2,1)}, u32[]{:S(2)}, u32[]{:S(2)}) collective-permute-start(bf16[2,128,640]{2,1,0:T(8,128)(2,1)S(1)} %collective-permute-done.9.refs_12_), channel_id=1, source_target_pairs={{0,224},{32,0},{64,32},{96,64},{128,96},{160,128},{192,160},{224,1... | collective-permute-start | bytes 983048 | tf_op jit(solution)/shard_map/ppermute | solution.py:176
  81.8 3.4 %collective-permute-done.6.refs_9_.up_ref = bf16[2,128,640]{2,1,0:T(8,128)(2,1)} collective-permute-done((bf16[2,128,640]{2,1,0:T(8,128)(2,1)S(1)}, bf16[2,128,640]{2,1,0:T(8,128)(2,1)}, u32[]{:S(2)}, u32[]{:S(2)}) %collective-permute-start.6) | collective-permute-done | bytes 327712 | tf_op jit(solution)/shard_map/ppermute | solution.py:176
  85.2 1.9 %collective-permute-start.7 = (bf16[2,128,640]{2,1,0:T(8,128)(2,1)}, bf16[2,128,640]{2,1,0:T(8,128)(2,1)}, u32[]{:S(2)}, u32[]{:S(2)}) collective-permute-start(bf16[2,128,640]{2,1,0:T(8,128)(2,1)} %collective-permute-done.6.refs_9_.up_ref), channel_id=1, source_target_pairs={{0,32},{32,64},{64,96},{96,128},{128,160},{160,192},{192,224},{224... | collective-permute-start | bytes 983048 | tf_op jit(solution)/shard_map/ppermute | solution.py:176
  87.2 0.0 all-to-all-done.1.parts_ref
  87.2 0.9 document_share.1
  88.1 6.6 %all-to-all-start.2 = ((f32[16,8,128]{2,1,0:T(8,128)}), f32[16,8,128]{2,1,0:T(8,128)S(1)}, u32[]{:S(2)}, u32[]{:S(2)}) async-start(f32[16,8,128]{2,1,0:T(8,128)} %get-tuple-element.16), calls=%async_computation.2 | async-start | bytes 131072 | tf_op jit(solution)/shard_map/all_to_all | solution.py:167
  94.7 0.0 collective-permute-done.7.refs_10_
  94.7 6.5 %input_gradient.1 = (bf16[8,128,256]{2,1,0:T(8,128)(2,1)S(1)}, bf16[8,128,256]{2,1,0:T(8,128)(2,1)}, bf16[8,128,256]{2,1,0:T(8,128)(2,1)}, bf16[8,128,256]{2,1,0:T(8,128)(2,1)}) custom-call(s32[5]{0:T(128)S(1)} %stack.23.place_ref, bf16[128,640]{1,0:T(8,128)(2,1)S(1)} %copy-done.1, bf16[128,640]{1,0:T(8,128)(2,1)S(1)} %collective-permute-done.refs_2_.refs_1_, ...), custom_call_target="tpu_custom_call" | custom-call | tf_op jit(solution)/shard_map/input_gradient/pallas_call | solution.py:244
  101.2 6.3 %collective-permute-start.11 = (bf16[8,128,256]{2,1,0:T(8,128)(2,1)}, bf16[8,128,256]{2,1,0:T(8,128)(2,1)S(1)}, u32[]{:S(2)}, u32[]{:S(2)}) collective-permute-start(bf16[8,128,256]{2,1,0:T(8,128)(2,1)} %get-tuple-element.12), channel_id=1, source_target_pairs={{0,16},{16,0},{1,17},{17,1},{2,18},{18,2},{3,19},{19,3},{4,20},{20... | collective-permute-start | bytes 1572872 | tf_op jit(solution)/shard_map/ppermute | solution.py:172
  107.4 3.2 %collective-permute-start.12 = (bf16[8,128,256]{2,1,0:T(8,128)(2,1)}, bf16[8,128,256]{2,1,0:T(8,128)(2,1)S(1)}, u32[]{:S(2)}, u32[]{:S(2)}) collective-permute-start(bf16[8,128,256]{2,1,0:T(8,128)(2,1)} %get-tuple-element.13), channel_id=1, source_target_pairs={{0,1},{1,0},{2,3},{3,2},{4,5},{5,4},{6,7},{7,6},{8,9},{9,8},{10,11... | collective-permute-start | bytes 1572872 | tf_op jit(solution)/shard_map/ppermute | solution.py:172
  110.6 2.3 %collective-permute-start.13 = (bf16[8,128,256]{2,1,0:T(8,128)(2,1)}, bf16[8,128,256]{2,1,0:T(8,128)(2,1)S(1)}, u32[]{:S(2)}, u32[]{:S(2)}) collective-permute-start(bf16[8,128,256]{2,1,0:T(8,128)(2,1)} %get-tuple-element.14), channel_id=1, source_target_pairs={{0,17},{1,16},{16,1},{17,0},{2,19},{3,18},{18,3},{19,2},{4,21},{5,... | collective-permute-start | bytes 1572872 | tf_op jit(solution)/shard_map/ppermute | solution.py:172
  113.0 23.5 %all_to_all.25.messages_ref = bf16[32,16,128]{2,1,0:T(8,128)(2,1)S(1)} all-to-all(bf16[32,16,128]{2,1,0:T(8,128)(2,1)S(1)} %document_messages.1), channel_id=1, replica_groups=mesh['xh'=2,'y'=8,'core'=2,'z'=8,'xl'=2] {'xh','y','core'}, dimensions={0} | all-to-all | bytes 262144 | tf_op jit(solution)/shard_map/all_to_all | solution.py:167
  136.4 0.8 clipped_sum.1
  137.2 8.8 %all-to-all-start.4 = ((bf16[32,16,128]{2,1,0:T(8,128)(2,1)}), bf16[32,16,128]{2,1,0:T(8,128)(2,1)S(1)}, u32[]{:S(2)}, u32[]{:S(2)}) async-start(bf16[32,16,128]{2,1,0:T(8,128)(2,1)} %clipped_sum.1), calls=%async_computation.4 | async-start | bytes 262144 | tf_op jit(solution)/shard_map/all_to_all | solution.py:167
  146.1 0.0 copy-start.3
  146.1 0.0 copy-start.5
  146.1 0.0 collective-permute-done.11.refs_1_
  146.1 0.0 collective-permute-done.13.refs_3_
  146.1 2.5 %interleave.1._ = bf16[128,8192]{1,0:T(8,128)(2,1)} custom-call(s32[5]{0:T(128)S(1)} %stack.23.place_ref, bf16[8,128,256]{2,1,0:T(8,128)(2,1)S(1)} %get-tuple-element.11.refs_0_._, bf16[8,128,256]{2,1,0:T(8,128)(2,1)S(1)} %collective-permute-done.11.refs_1_, bf16[8,128,256]{2,1,0:T(8,128)(2,1)S(1)} %collective-permute-done.12.refs_2_, ...), custom_call_target="tpu_custom_call" | custom-call | tf_op jit(solution)/shard_map/interleave/pallas_call | solution.py:255
  148.6 8.0 %all-to-all-done.4.tiles_ref = bf16[32,16,128]{2,1,0:T(8,128)(2,1)S(1)} async-done(((bf16[32,16,128]{2,1,0:T(8,128)(2,1)}), bf16[32,16,128]{2,1,0:T(8,128)(2,1)S(1)}, u32[]{:S(2)}, u32[]{:S(2)}) %all-to-all-start.4) | async-done | bytes 131104 | tf_op jit(solution)/shard_map/all_to_all | solution.py:167
  156.7 0.8 finish.1
  (23 shorter events, 0.1 us)
Async XLA Ops:
  0.6 11.9 %copy-start = (bf16[256,640]{1,0:T(8,128)(2,1)S(1)}, bf16[256,640]{1,0:T(8,128)(2,1)}, u32[]{:S(2)}) copy-start(bf16[256,640]{1,0:T(8,128)(2,1)} %param.9) | copy-start | bytes 983044
  0.6 0.8 copy-start.4
  2.3 30.8 %all-to-all-start = ((bf16[16,64,256]{2,1,0:T(8,128)(2,1)}), bf16[16,64,256]{2,1,0:T(8,128)(2,1)S(1)}, u32[]{:S(2)}, u32[]{:S(2)}) async-start(bf16[16,64,256]{2,1,0:T(8,128)(2,1)} %copies.1), calls=%async_computation | async-start | bytes 1048576 | tf_op jit(solution)/shard_map/all_to_all | solution.py:167
  12.5 13.5 %collective-permute-start.3 = (bf16[128,640]{1,0:T(8,128)(2,1)S(1)}, bf16[128,640]{1,0:T(8,128)(2,1)S(1)}, u32[]{:S(2)}, u32[]{:S(2)}) collective-permute-start(bf16[128,640]{1,0:T(8,128)(2,1)S(1)} %constant_dynamic-slice_fusion.own_ref), channel_id=1, source_target_pairs={{0,256},{256,0},{1,257},{257,1},{2,258},{258,2},{3,259},{259,3},{4... | collective-permute-start | bytes 491528 | tf_op jit(solution)/shard_map/ppermute | solution.py:172
  17.3 12.9 %collective-permute-start.2 = (bf16[128,640]{1,0:T(8,128)(2,1)}, bf16[128,640]{1,0:T(8,128)(2,1)S(1)}, u32[]{:S(2)}, u32[]{:S(2)}) collective-permute-start(bf16[128,640]{1,0:T(8,128)(2,1)} %g_ref.1), channel_id=1, source_target_pairs={{0,17},{1,16},{16,1},{17,0},{2,19},{3,18},{18,3},{19,2},{4,21},{5,... | collective-permute-start | bytes 491528 | tf_op jit(solution)/shard_map/ppermute | solution.py:172
  21.0 12.1 %collective-permute-start.1 = (bf16[128,640]{1,0:T(8,128)(2,1)}, bf16[128,640]{1,0:T(8,128)(2,1)S(1)}, u32[]{:S(2)}, u32[]{:S(2)}) collective-permute-start(bf16[128,640]{1,0:T(8,128)(2,1)} %g_ref.1), channel_id=1, source_target_pairs={{0,1},{1,0},{2,3},{3,2},{4,5},{5,4},{6,7},{7,6},{8,9},{9,8},{10,11... | collective-permute-start | bytes 491528 | tf_op jit(solution)/shard_map/ppermute | solution.py:172
  24.0 9.0 %collective-permute-start = (bf16[128,640]{1,0:T(8,128)(2,1)}, bf16[128,640]{1,0:T(8,128)(2,1)S(1)}, u32[]{:S(2)}, u32[]{:S(2)}) collective-permute-start(bf16[128,640]{1,0:T(8,128)(2,1)} %g_ref.1), channel_id=1, source_target_pairs={{0,16},{16,0},{1,17},{17,1},{2,18},{18,2},{3,19},{19,3},{4,20},{20... | collective-permute-start | bytes 491528 | tf_op jit(solution)/shard_map/ppermute | solution.py:172
  33.1 4.3 %collective-permute-start.14 = (bf16[16,64,256]{2,1,0:T(8,128)(2,1)S(1)}, bf16[16,64,256]{2,1,0:T(8,128)(2,1)S(1)}, u32[]{:S(2)}, u32[]{:S(2)}) collective-permute-start(bf16[16,64,256]{2,1,0:T(8,128)(2,1)S(1)} %wait.1.refs_5_.own_ref), channel_id=1, source_target_pairs={{0,16},{16,0},{1,17},{17,1},{2,18},{18,2},{3,19},{19,3},{4,20},{20... | collective-permute-start | bytes 1572872 | tf_op jit(solution)/shard_map/ppermute | solution.py:172
  41.7 53.0 %copy-start.1 = (bf16[128,640]{1,0:T(8,128)(2,1)S(1)}, bf16[128,640]{1,0:T(8,128)(2,1)}, u32[]{:S(2)}) copy-start(bf16[128,640]{1,0:T(8,128)(2,1)} %g_ref.1) | copy-start | bytes 491524
  41.7 53.0 %copy-start.2 = (bf16[64,640]{1,0:T(8,128)(2,1)S(1)}, bf16[64,640]{1,0:T(8,128)(2,1)}, u32[]{:S(2)}) copy-start(bf16[64,640]{1,0:T(8,128)(2,1)} %b_ref.1) | copy-start | bytes 245764
  41.7 45.5 %all-to-all-start.1 = ((bf16[16,72,512]{2,1,0:T(8,128)(2,1)}), bf16[16,72,512]{2,1,0:T(8,128)(2,1)S(1)}, u32[]{:S(2)}, u32[]{:S(2)}) async-start(bf16[16,72,512]{2,1,0:T(8,128)(2,1)} %partials.1), calls=%async_computation.1 | async-start | bytes 2359296 | tf_op jit(solution)/shard_map/all_to_all | solution.py:167
  52.8 11.7 %collective-permute-start.4 = (bf16[2,128,640]{2,1,0:T(8,128)(2,1)S(1)}, bf16[2,128,640]{2,1,0:T(8,128)(2,1)S(1)}, u32[]{:S(2)}, u32[]{:S(2)}) collective-permute-start(bf16[2,128,640]{2,1,0:T(8,128)(2,1)S(1)} %own_rows.1.refs_1_.refs_6_), channel_id=1, source_target_pairs={{0,32},{32,64},{64,96},{96,128},{128,160},{160,192},{192,224},{224... | collective-permute-start | bytes 983048 | tf_op jit(solution)/shard_map/ppermute | solution.py:176
  55.8 10.7 %collective-permute-start.8 = (bf16[2,128,640]{2,1,0:T(8,128)(2,1)S(1)}, bf16[2,128,640]{2,1,0:T(8,128)(2,1)S(1)}, u32[]{:S(2)}, u32[]{:S(2)}) collective-permute-start(bf16[2,128,640]{2,1,0:T(8,128)(2,1)S(1)} %own_rows.1.refs_1_.refs_6_), channel_id=1, source_target_pairs={{0,224},{32,0},{64,32},{96,64},{128,96},{160,128},{192,160},{224,1... | collective-permute-start | bytes 983048 | tf_op jit(solution)/shard_map/ppermute | solution.py:176
  64.5 22.6 %copy-start.6 = (bf16[2,128,640]{2,1,0:T(8,128)(2,1)}, bf16[2,128,640]{2,1,0:T(8,128)(2,1)S(1)}, u32[]{:S(2)}) copy-start(bf16[2,128,640]{2,1,0:T(8,128)(2,1)S(1)} %collective-permute-done.4.refs_7_) | copy-start | bytes 983044
  64.5 10.8 %collective-permute-start.5 = (bf16[2,128,640]{2,1,0:T(8,128)(2,1)S(1)}, bf16[2,128,640]{2,1,0:T(8,128)(2,1)S(1)}, u32[]{:S(2)}, u32[]{:S(2)}) collective-permute-start(bf16[2,128,640]{2,1,0:T(8,128)(2,1)S(1)} %collective-permute-done.4.refs_7_), channel_id=1, source_target_pairs={{0,32},{32,64},{64,96},{96,128},{128,160},{160,192},{192,224},{224... | collective-permute-start | bytes 983048 | tf_op jit(solution)/shard_map/ppermute | solution.py:176
  66.4 20.7 %copy-start.7 = (bf16[2,128,640]{2,1,0:T(8,128)(2,1)}, bf16[2,128,640]{2,1,0:T(8,128)(2,1)S(1)}, u32[]{:S(2)}) copy-start(bf16[2,128,640]{2,1,0:T(8,128)(2,1)S(1)} %collective-permute-done.8.refs_13_) | copy-start | bytes 983044
  66.4 10.7 %collective-permute-start.9 = (bf16[2,128,640]{2,1,0:T(8,128)(2,1)S(1)}, bf16[2,128,640]{2,1,0:T(8,128)(2,1)S(1)}, u32[]{:S(2)}, u32[]{:S(2)}) collective-permute-start(bf16[2,128,640]{2,1,0:T(8,128)(2,1)S(1)} %collective-permute-done.8.refs_13_), channel_id=1, source_target_pairs={{0,224},{32,0},{64,32},{96,64},{128,96},{160,128},{192,160},{224,1... | collective-permute-start | bytes 983048 | tf_op jit(solution)/shard_map/ppermute | solution.py:176
  75.3 11.9 %copy-start.8 = (bf16[2,128,640]{2,1,0:T(8,128)(2,1)}, bf16[2,128,640]{2,1,0:T(8,128)(2,1)S(1)}, u32[]{:S(2)}) copy-start(bf16[2,128,640]{2,1,0:T(8,128)(2,1)S(1)} %collective-permute-done.5.refs_8_) | copy-start | bytes 983044
  75.3 9.9 %collective-permute-start.6 = (bf16[2,128,640]{2,1,0:T(8,128)(2,1)S(1)}, bf16[2,128,640]{2,1,0:T(8,128)(2,1)}, u32[]{:S(2)}, u32[]{:S(2)}) collective-permute-start(bf16[2,128,640]{2,1,0:T(8,128)(2,1)S(1)} %collective-permute-done.5.refs_8_), channel_id=1, source_target_pairs={{0,32},{32,64},{64,96},{96,128},{128,160},{160,192},{192,224},{224... | collective-permute-start | bytes 983048 | tf_op jit(solution)/shard_map/ppermute | solution.py:176
  77.2 10.0 %copy-start.9 = (bf16[2,128,640]{2,1,0:T(8,128)(2,1)}, bf16[2,128,640]{2,1,0:T(8,128)(2,1)S(1)}, u32[]{:S(2)}) copy-start(bf16[2,128,640]{2,1,0:T(8,128)(2,1)S(1)} %collective-permute-done.9.refs_12_) | copy-start | bytes 983044
  77.2 10.0 %collective-permute-start.10 = (bf16[2,128,640]{2,1,0:T(8,128)(2,1)S(1)}, bf16[2,128,640]{2,1,0:T(8,128)(2,1)}, u32[]{:S(2)}, u32[]{:S(2)}) collective-permute-start(bf16[2,128,640]{2,1,0:T(8,128)(2,1)S(1)} %collective-permute-done.9.refs_12_), channel_id=1, source_target_pairs={{0,224},{32,0},{64,32},{96,64},{128,96},{160,128},{192,160},{224,1... | collective-permute-start | bytes 983048 | tf_op jit(solution)/shard_map/ppermute | solution.py:176
  85.2 9.5 %collective-permute-start.7 = (bf16[2,128,640]{2,1,0:T(8,128)(2,1)}, bf16[2,128,640]{2,1,0:T(8,128)(2,1)}, u32[]{:S(2)}, u32[]{:S(2)}) collective-permute-start(bf16[2,128,640]{2,1,0:T(8,128)(2,1)} %collective-permute-done.6.refs_9_.up_ref), channel_id=1, source_target_pairs={{0,32},{32,64},{64,96},{96,128},{128,160},{160,192},{192,224},{224... | collective-permute-start | bytes 983048 | tf_op jit(solution)/shard_map/ppermute | solution.py:176
  88.1 24.8 %all-to-all-start.2 = ((f32[16,8,128]{2,1,0:T(8,128)}), f32[16,8,128]{2,1,0:T(8,128)S(1)}, u32[]{:S(2)}, u32[]{:S(2)}) async-start(f32[16,8,128]{2,1,0:T(8,128)} %get-tuple-element.16), calls=%async_computation.2 | async-start | bytes 131072 | tf_op jit(solution)/shard_map/all_to_all | solution.py:167
  101.2 44.9 %collective-permute-start.11 = (bf16[8,128,256]{2,1,0:T(8,128)(2,1)}, bf16[8,128,256]{2,1,0:T(8,128)(2,1)S(1)}, u32[]{:S(2)}, u32[]{:S(2)}) collective-permute-start(bf16[8,128,256]{2,1,0:T(8,128)(2,1)} %get-tuple-element.12), channel_id=1, source_target_pairs={{0,16},{16,0},{1,17},{17,1},{2,18},{18,2},{3,19},{19,3},{4,20},{20... | collective-permute-start | bytes 1572872 | tf_op jit(solution)/shard_map/ppermute | solution.py:172
  107.4 38.7 %collective-permute-start.12 = (bf16[8,128,256]{2,1,0:T(8,128)(2,1)}, bf16[8,128,256]{2,1,0:T(8,128)(2,1)S(1)}, u32[]{:S(2)}, u32[]{:S(2)}) collective-permute-start(bf16[8,128,256]{2,1,0:T(8,128)(2,1)} %get-tuple-element.13), channel_id=1, source_target_pairs={{0,1},{1,0},{2,3},{3,2},{4,5},{5,4},{6,7},{7,6},{8,9},{9,8},{10,11... | collective-permute-start | bytes 1572872 | tf_op jit(solution)/shard_map/ppermute | solution.py:172
  110.6 35.5 %collective-permute-start.13 = (bf16[8,128,256]{2,1,0:T(8,128)(2,1)}, bf16[8,128,256]{2,1,0:T(8,128)(2,1)S(1)}, u32[]{:S(2)}, u32[]{:S(2)}) collective-permute-start(bf16[8,128,256]{2,1,0:T(8,128)(2,1)} %get-tuple-element.14), channel_id=1, source_target_pairs={{0,17},{1,16},{16,1},{17,0},{2,19},{3,18},{18,3},{19,2},{4,21},{5,... | collective-permute-start | bytes 1572872 | tf_op jit(solution)/shard_map/ppermute | solution.py:172
  137.2 19.4 %all-to-all-start.4 = ((bf16[32,16,128]{2,1,0:T(8,128)(2,1)}), bf16[32,16,128]{2,1,0:T(8,128)(2,1)S(1)}, u32[]{:S(2)}, u32[]{:S(2)}) async-start(bf16[32,16,128]{2,1,0:T(8,128)(2,1)} %clipped_sum.1), calls=%async_computation.4 | async-start | bytes 262144 | tf_op jit(solution)/shard_map/all_to_all | solution.py:167
  146.1 10.6 %copy-start.3 = (f32[512,64]{0,1:T(8,128)S(1)}, f32[512,64]{0,1:T(8,128)}, u32[]{:S(2)}) copy-start(f32[512,64]{0,1:T(8,128)} %param.12) | copy-start | bytes 393220
  146.1 10.6 %copy-start.5 = (f32[64,40]{0,1:T(8,128)S(1)}, f32[64,40]{0,1:T(8,128)}, u32[]{:S(2)}) copy-start(f32[64,40]{0,1:T(8,128)} %param.13) | copy-start | bytes 30724

commit v3 on v2

--- a/solution.py
+++ b/solution.py
@@ -86,7 +86,7 @@
         square_ref[j] = square
 
 
-def document_messages_kernel(share_ref, squares_ref, _, out_ref):
+def document_messages_kernel(share_ref, squares_ref, out_ref):
     square = squares_ref[0]
     for j in range(1, CTX):
         square += squares_ref[j]
@@ -100,7 +100,8 @@
         out_ref[k] = jnp.concatenate([tile, tail], axis=0).astype(BF16)
 
 
-def clipped_sum_kernel(messages_ref, out_ref):
+def clipped_sum_kernel(messages_ref, *refs):
+    out_ref = refs[2]
     norms = messages_ref[:, 9, :].astype(F32) + messages_ref[:, 10, :].astype(F32) + messages_ref[:, 11, :].astype(F32)
     bound = jnp.sum(norms, axis=0, keepdims=True) / DOCS
     factor = bound / jnp.maximum(norms, bound)
@@ -193,7 +194,7 @@
         out_shape=pltpu.VMEM((16, 64, 256), BF16),
         compiler_params=VMEM_LIMIT,
         name="copies",
-    )(adapter_first_factor.T)
+    )(*in_hbm(adapter_first_factor.T))
     factor_t = exchange(factor_t, ("xh", "y"))
 
     gradients = [swap(key_output_gradient, axes) for axes in ("core", "xl", ("core", "xl"))]
@@ -244,38 +245,38 @@
     products = pl.pallas_call(
         input_gradient_kernel,
         in_specs=[SMEM] + [VMEM] * 14,
-        out_shape=[jax.ShapeDtypeStruct((8, 128, 256), BF16)] * 4,
+        out_shape=[pltpu.HBM((8, 128, 256), BF16)] * 4,
         compiler_params=VMEM_LIMIT,
         name="input_gradient",
     )(place, key_output_gradient, *in_vmem(*gradients), adapter_second_factor, *in_vmem(factor_t, near), *in_hbm(*blocks[1:]))
-    own = products[0]
-    products = [own] + [
-        swap(product, axes) for product, axes in zip(products[1:], ("core", "xl", ("core", "xl")))
-    ]
+    xl_product = swap(products[2], "xl")
+    messages = pl.pallas_call(
+        document_messages_kernel,
+        in_specs=[VMEM] * 2,
+        out_shape=pltpu.VMEM((DOCS, 16, 128), BF16),
+        compiler_params=VMEM_LIMIT,
+        name="document_messages",
+    )(*in_vmem(share, squares))
+    messages = exchange(messages, DP_PARTS)
+
+    tiles, *theirs = pl.pallas_call(
+        clipped_sum_kernel,
+        in_specs=[VMEM] + [ANY] * 2,
+        out_specs=[VMEM] + [ANY] * 2,
+        out_shape=[pltpu.VMEM((DOCS, 16, 128), BF16)] + [pltpu.HBM((8, 128, 256), BF16)] * 2,
+        input_output_aliases={1: 1, 2: 2},
+        compiler_params=VMEM_LIMIT,
+        name="clipped_sum",
+    )(*in_vmem(messages), *in_hbm(products[1], products[3]))
+    products = [products[0], swap(theirs[0], "core"), xl_product, swap(theirs[1], ("core", "xl"))]
     d_input = pl.pallas_call(
         interleave_kernel,
         in_specs=[SMEM] + [VMEM] * 4,
         out_shape=pltpu.HBM((128, 8192), BF16),
         compiler_params=VMEM_LIMIT,
         name="interleave",
-    )(place, products[0], *in_vmem(*products[1:]))
-
-    messages = pl.pallas_call(
-        document_messages_kernel,
-        in_specs=[VMEM, VMEM, ANY],
-        out_shape=pltpu.VMEM((DOCS, 16, 128), BF16),
-        compiler_params=VMEM_LIMIT,
-        name="document_messages",
-    )(*in_vmem(share, squares), own)
-    messages = exchange(messages, DP_PARTS)
-
-    tiles = pl.pallas_call(
-        clipped_sum_kernel,
-        in_specs=[VMEM],
-        out_shape=pltpu.VMEM((DOCS, 16, 128), BF16),
-        compiler_params=VMEM_LIMIT,
-        name="clipped_sum",
-    )(*in_vmem(messages))
+    )(place, *in_hbm(products[0]), *in_vmem(*products[1:]))
+
     tiles = exchange(tiles, DP_PARTS)
 
     grad_a, grad_b = pl.pallas_call(

time: 158 us -> 157 us (level)
  blocking collectives: 23.5 us -> 0 us
  waiting for transfers between devices: 28.8 us -> 40.4 us
  starting transfers between devices: 86 us -> 93.4 us
  Pallas kernels: 17.1 us -> 19.3 us
    all_to_all x1 -> x0, blocking collectives: 23.5 us -> none  [exchange(): return lax.all_to_all(pieces, axes, 0, 0)]
    all_to_all x4 -> x5, starting transfers between devices: 36.8 us -> 47.8 us  [exchange(): return lax.all_to_all(pieces, axes, 0, 0)]
    ppermute x8, waiting for transfers between devices: 7.94 us -> 18 us  [swap(): lax.ppermute(array, axes, [(at, count - 1 - at) for at in range(count)])]
    ppermute x8, starting transfers between devices: 27.9 us -> 23.5 us  [swap(): lax.ppermute(array, axes, [(at, count - 1 - at) for at in range(count)])]
    ppermute x7, waiting for transfers between devices: 12.8 us -> 15.1 us  [shift(): return lax.ppermute(array, axis, [(at, (at + by) % 8) for at in range(8)])]
    all_to_all x4 -> x5, waiting for transfers between devices: 8.04 us -> 7.32 us  [exchange(): return lax.all_to_all(pieces, axes, 0, 0)]
  transfers between devices with their start and end apart: 19 -> 20, of which waited for: 7 -> 10; matrix products, arithmetic and copies ran while one was open for 0% -> 0% of each run, Pallas kernels for 7% -> 7%
where the time goes in v3:
time: 157 us; the launch traced here: 156 us
  starting transfers between devices  93.4 us (59%)
  waiting for transfers between devices  40.4 us (26%)
  Pallas kernels  19.3 us (12%)
  local copies, waits for them, and re-layouts  1.6 us (1%)
    all_to_all x5, starting transfers between devices, exchange(): return lax.all_to_all(pieces, axes, 0, 0)  47.8 us
    ppermute x8, starting transfers between devices, swap(): lax.ppermute(array, axes, [(at, count - 1 - at) for at in range(count)])  23.5 us
    ppermute x7, starting transfers between devices, shift(): return lax.ppermute(array, axis, [(at, (at + by) % 8) for at in range(8)])  22.1 us
    ppermute x8, waiting for transfers between devices, swap(): lax.ppermute(array, axes, [(at, count - 1 - at) for at in range(count)])  18 us
    ppermute x7, waiting for transfers between devices, shift(): return lax.ppermute(array, axis, [(at, (at + by) % 8) for at in range(8)])  15.1 us
    all_to_all x5, waiting for transfers between devices, exchange(): return lax.all_to_all(pieces, axes, 0, 0)  7.32 us
    pallas_call x1, Pallas kernels, per_device(): pl.pallas_call(input_gradient_kernel, in_specs=[SMEM] + [VMEM] * 14, out_...  6.57 us
    pallas_call x1, Pallas kernels, per_device(): pl.pallas_call(partials_kernel, in_specs=[SMEM] + [VMEM] * 5, out_shape=p...  4.29 us
  transfers between devices with their start and end apart: 20, of which 10 were waited for; matrix products, arithmetic and copies ran while one was open for 0% of the time, Pallas kernels for 7%

profile of v3, /device:TPU:1, one launch (start us, length us, event | category | flops | bytes accessed | tf_op | source)
XLA Modules:
  0.0 155.6 jit_solution(12647850282332587029)
XLA Ops:
  0.6 0.0 copy-start
  0.6 1.6 %copies.1 = bf16[16,64,256]{2,1,0:T(8,128)(2,1)} custom-call(bf16[64,256]{1,0:T(8,128)(2,1)} %bitcast.12), custom_call_target="tpu_custom_call" | custom-call | tf_op jit(solution)/shard_map/copies/pallas_call | solution.py:191
  2.3 10.2 %all-to-all-start = ((bf16[16,64,256]{2,1,0:T(8,128)(2,1)}), bf16[16,64,256]{2,1,0:T(8,128)(2,1)S(1)}, u32[]{:S(2)}, u32[]{:S(2)}) async-start(bf16[16,64,256]{2,1,0:T(8,128)(2,1)} %copies.1), calls=%async_computation | async-start | bytes 1048576 | tf_op jit(solution)/shard_map/all_to_all | solution.py:168
  12.5 4.8 %collective-permute-start.3 = (bf16[128,640]{1,0:T(8,128)(2,1)S(1)}, bf16[128,640]{1,0:T(8,128)(2,1)S(1)}, u32[]{:S(2)}, u32[]{:S(2)}) collective-permute-start(bf16[128,640]{1,0:T(8,128)(2,1)S(1)} %constant_dynamic-slice_fusion.own_ref), channel_id=1, source_target_pairs={{0,256},{256,0},{1,257},{257,1},{2,258},{258,2},{3,259},{259,3},{4... | collective-permute-start | bytes 491528 | tf_op jit(solution)/shard_map/ppermute | solution.py:173
  17.3 3.6 %collective-permute-start.2 = (bf16[128,640]{1,0:T(8,128)(2,1)}, bf16[128,640]{1,0:T(8,128)(2,1)S(1)}, u32[]{:S(2)}, u32[]{:S(2)}) collective-permute-start(bf16[128,640]{1,0:T(8,128)(2,1)} %g_ref.1), channel_id=1, source_target_pairs={{0,17},{1,16},{16,1},{17,0},{2,19},{3,18},{18,3},{19,2},{4,21},{5,... | collective-permute-start | bytes 491528 | tf_op jit(solution)/shard_map/ppermute | solution.py:173
  21.0 3.1 %collective-permute-start.1 = (bf16[128,640]{1,0:T(8,128)(2,1)}, bf16[128,640]{1,0:T(8,128)(2,1)S(1)}, u32[]{:S(2)}, u32[]{:S(2)}) collective-permute-start(bf16[128,640]{1,0:T(8,128)(2,1)} %g_ref.1), channel_id=1, source_target_pairs={{0,1},{1,0},{2,3},{3,2},{4,5},{5,4},{6,7},{7,6},{8,9},{9,8},{10,11... | collective-permute-start | bytes 491528 | tf_op jit(solution)/shard_map/ppermute | solution.py:173
  24.0 1.9 %collective-permute-start = (bf16[128,640]{1,0:T(8,128)(2,1)}, bf16[128,640]{1,0:T(8,128)(2,1)S(1)}, u32[]{:S(2)}, u32[]{:S(2)}) collective-permute-start(bf16[128,640]{1,0:T(8,128)(2,1)} %g_ref.1), channel_id=1, source_target_pairs={{0,16},{16,0},{1,17},{17,1},{2,18},{18,2},{3,19},{19,3},{4,20},{20... | collective-permute-start | bytes 491528 | tf_op jit(solution)/shard_map/ppermute | solution.py:173
  26.0 0.1 stack.23.place_ref
  26.0 0.0 collective-permute-done.3.other_ref
  26.1 0.6 own_rows.1.refs_1_.refs_6_
  26.6 3.6 %collective-permute-done.2.refs_4_.refs_3_ = bf16[128,640]{1,0:T(8,128)(2,1)S(1)} collective-permute-done((bf16[128,640]{1,0:T(8,128)(2,1)}, bf16[128,640]{1,0:T(8,128)(2,1)S(1)}, u32[]{:S(2)}, u32[]{:S(2)}) %collective-permute-start.2) | collective-permute-done | bytes 163872 | tf_op jit(solution)/shard_map/ppermute | solution.py:173
  30.3 2.8 %collective-permute-done.1.refs_3_.refs_2_ = bf16[128,640]{1,0:T(8,128)(2,1)S(1)} collective-permute-done((bf16[128,640]{1,0:T(8,128)(2,1)}, bf16[128,640]{1,0:T(8,128)(2,1)S(1)}, u32[]{:S(2)}, u32[]{:S(2)}) %collective-permute-start.1) | collective-permute-done | bytes 163872 | tf_op jit(solution)/shard_map/ppermute | solution.py:173
  33.0 0.0 collective-permute-done.refs_2_.refs_1_
  33.1 2.8 %collective-permute-start.11 = (bf16[16,64,256]{2,1,0:T(8,128)(2,1)S(1)}, bf16[16,64,256]{2,1,0:T(8,128)(2,1)S(1)}, u32[]{:S(2)}, u32[]{:S(2)}) collective-permute-start(bf16[16,64,256]{2,1,0:T(8,128)(2,1)S(1)} %wait.1.refs_5_.own_ref), channel_id=1, source_target_pairs={{0,16},{16,0},{1,17},{17,1},{2,18},{18,2},{3,19},{19,3},{4,20},{20... | collective-permute-start | bytes 1572872 | tf_op jit(solution)/shard_map/ppermute | solution.py:173
  35.8 1.5 collective-permute-done.11.other_ref
  37.4 4.3 %partials.1 = bf16[16,72,512]{2,1,0:T(8,128)(2,1)} custom-call(s32[5]{0:T(128)S(1)} %stack.23.place_ref, bf16[128,8192]{1,0:T(8,128)(2,1)} %x_ref.1, bf16[128,640]{1,0:T(8,128)(2,1)} %g_ref.1, bf16[64,640]{1,0:T(8,128)(2,1)} %b_ref.1, bf16[16,64,256]{2,1,0:T(8,128)(2,1)S(1)} %wait.1.refs_5_.own_ref, bf16[16,64,256]{2,1,0:T(8,128)(2,1)S(1)} %collective-permute-done.11.other_ref), custom_call_target="tpu_custom_call" | custom-call | tf_op jit(solution)/shard_map/partials/pallas_call | solution.py:217
  41.7 11.1 %all-to-all-start.1 = ((bf16[16,72,512]{2,1,0:T(8,128)(2,1)}), bf16[16,72,512]{2,1,0:T(8,128)(2,1)S(1)}, u32[]{:S(2)}, u32[]{:S(2)}) async-start(bf16[16,72,512]{2,1,0:T(8,128)(2,1)} %partials.1), calls=%async_computation.1 | async-start | bytes 2359296 | tf_op jit(solution)/shard_map/all_to_all | solution.py:168
  52.8 4.0 %collective-permute-start.8 = (bf16[2,128,640]{2,1,0:T(8,128)(2,1)S(1)}, bf16[2,128,640]{2,1,0:T(8,128)(2,1)S(1)}, u32[]{:S(2)}, u32[]{:S(2)}) collective-permute-start(bf16[2,128,640]{2,1,0:T(8,128)(2,1)S(1)} %own_rows.1.refs_1_.refs_6_), channel_id=1, source_target_pairs={{0,224},{32,0},{64,32},{96,64},{128,96},{160,128},{192,160},{224,1... | collective-permute-start | bytes 983048 | tf_op jit(solution)/shard_map/ppermute | solution.py:177
  56.8 1.9 %collective-permute-start.4 = (bf16[2,128,640]{2,1,0:T(8,128)(2,1)S(1)}, bf16[2,128,640]{2,1,0:T(8,128)(2,1)S(1)}, u32[]{:S(2)}, u32[]{:S(2)}) collective-permute-start(bf16[2,128,640]{2,1,0:T(8,128)(2,1)S(1)} %own_rows.1.refs_1_.refs_6_), channel_id=1, source_target_pairs={{0,32},{32,64},{64,96},{96,128},{128,160},{160,192},{192,224},{224... | collective-permute-start | bytes 983048 | tf_op jit(solution)/shard_map/ppermute | solution.py:177
  58.7 4.6 %collective-permute-done.8.refs_13_ = bf16[2,128,640]{2,1,0:T(8,128)(2,1)S(1)} collective-permute-done((bf16[2,128,640]{2,1,0:T(8,128)(2,1)S(1)}, bf16[2,128,640]{2,1,0:T(8,128)(2,1)S(1)}, u32[]{:S(2)}, u32[]{:S(2)}) %collective-permute-start.8) | collective-permute-done | bytes 327712 | tf_op jit(solution)/shard_map/ppermute | solution.py:177
  63.3 5.2 %collective-permute-start.9 = (bf16[2,128,640]{2,1,0:T(8,128)(2,1)S(1)}, bf16[2,128,640]{2,1,0:T(8,128)(2,1)S(1)}, u32[]{:S(2)}, u32[]{:S(2)}) collective-permute-start(bf16[2,128,640]{2,1,0:T(8,128)(2,1)S(1)} %collective-permute-done.8.refs_13_), channel_id=1, source_target_pairs={{0,224},{32,0},{64,32},{96,64},{128,96},{160,128},{192,160},{224,1... | collective-permute-start | bytes 983048 | tf_op jit(solution)/shard_map/ppermute | solution.py:177
  68.5 1.9 %collective-permute-start.5 = (bf16[2,128,640]{2,1,0:T(8,128)(2,1)S(1)}, bf16[2,128,640]{2,1,0:T(8,128)(2,1)S(1)}, u32[]{:S(2)}, u32[]{:S(2)}) collective-permute-start(bf16[2,128,640]{2,1,0:T(8,128)(2,1)S(1)} %collective-permute-done.4.refs_7_), channel_id=1, source_target_pairs={{0,32},{32,64},{64,96},{96,128},{128,160},{160,192},{192,224},{224... | collective-permute-start | bytes 983048 | tf_op jit(solution)/shard_map/ppermute | solution.py:177
  70.4 3.5 %collective-permute-done.9.refs_12_ = bf16[2,128,640]{2,1,0:T(8,128)(2,1)S(1)} collective-permute-done((bf16[2,128,640]{2,1,0:T(8,128)(2,1)S(1)}, bf16[2,128,640]{2,1,0:T(8,128)(2,1)S(1)}, u32[]{:S(2)}, u32[]{:S(2)}) %collective-permute-start.9) | collective-permute-done | bytes 327712 | tf_op jit(solution)/shard_map/ppermute | solution.py:177
  73.9 5.3 %collective-permute-start.10 = (bf16[2,128,640]{2,1,0:T(8,128)(2,1)S(1)}, bf16[2,128,640]{2,1,0:T(8,128)(2,1)S(1)}, u32[]{:S(2)}, u32[]{:S(2)}) collective-permute-start(bf16[2,128,640]{2,1,0:T(8,128)(2,1)S(1)} %collective-permute-done.9.refs_12_), channel_id=1, source_target_pairs={{0,224},{32,0},{64,32},{96,64},{128,96},{160,128},{192,160},{224,1... | collective-permute-start | bytes 983048 | tf_op jit(solution)/shard_map/ppermute | solution.py:177
  79.2 0.0 collective-permute-done.5.refs_8_
  79.2 1.9 %collective-permute-start.6 = (bf16[2,128,640]{2,1,0:T(8,128)(2,1)S(1)}, bf16[2,128,640]{2,1,0:T(8,128)(2,1)}, u32[]{:S(2)}, u32[]{:S(2)}) collective-permute-start(bf16[2,128,640]{2,1,0:T(8,128)(2,1)S(1)} %collective-permute-done.5.refs_8_), channel_id=1, source_target_pairs={{0,32},{32,64},{64,96},{96,128},{128,160},{160,192},{192,224},{224... | collective-permute-start | bytes 983048 | tf_op jit(solution)/shard_map/ppermute | solution.py:177
  81.2 2.6 %collective-permute-done.10.refs_11_.down_ref = bf16[2,128,640]{2,1,0:T(8,128)(2,1)S(1)} collective-permute-done((bf16[2,128,640]{2,1,0:T(8,128)(2,1)S(1)}, bf16[2,128,640]{2,1,0:T(8,128)(2,1)S(1)}, u32[]{:S(2)}, u32[]{:S(2)}) %collective-permute-start.10) | collective-permute-done | bytes 327712 | tf_op jit(solution)/shard_map/ppermute | solution.py:177
  83.8 0.7 copy-done.5
  84.5 4.4 %collective-permute-done.6.refs_9_.up_ref = bf16[2,128,640]{2,1,0:T(8,128)(2,1)} collective-permute-done((bf16[2,128,640]{2,1,0:T(8,128)(2,1)S(1)}, bf16[2,128,640]{2,1,0:T(8,128)(2,1)}, u32[]{:S(2)}, u32[]{:S(2)}) %collective-permute-start.6) | collective-permute-done | bytes 327712 | tf_op jit(solution)/shard_map/ppermute | solution.py:177
  88.9 0.0 all-to-all-done.1.parts_ref
  88.9 0.9 document_share.1
  89.8 6.4 %all-to-all-start.2 = ((f32[16,8,128]{2,1,0:T(8,128)}), f32[16,8,128]{2,1,0:T(8,128)S(1)}, u32[]{:S(2)}, u32[]{:S(2)}) async-start(f32[16,8,128]{2,1,0:T(8,128)} %get-tuple-element.16), calls=%async_computation.2 | async-start | bytes 131072 | tf_op jit(solution)/shard_map/all_to_all | solution.py:168
  96.2 1.9 %collective-permute-start.7 = (bf16[2,128,640]{2,1,0:T(8,128)(2,1)}, bf16[2,128,640]{2,1,0:T(8,128)(2,1)S(1)}, u32[]{:S(2)}, u32[]{:S(2)}) collective-permute-start(bf16[2,128,640]{2,1,0:T(8,128)(2,1)} %collective-permute-done.6.refs_9_.up_ref), channel_id=1, source_target_pairs={{0,32},{32,64},{64,96},{96,128},{128,160},{160,192},{192,224},{224... | collective-permute-start | bytes 983048 | tf_op jit(solution)/shard_map/ppermute | solution.py:177
  98.1 6.0 %all-to-all-done.2.squares_ref = f32[16,8,128]{2,1,0:T(8,128)S(1)} async-done(((f32[16,8,128]{2,1,0:T(8,128)}), f32[16,8,128]{2,1,0:T(8,128)S(1)}, u32[]{:S(2)}, u32[]{:S(2)}) %all-to-all-start.2) | async-done | bytes 65568 | tf_op jit(solution)/shard_map/all_to_all | solution.py:168
  104.1 0.7 document_messages.1
  104.8 11.1 %all-to-all-start.3 = ((bf16[32,16,128]{2,1,0:T(8,128)(2,1)}), bf16[32,16,128]{2,1,0:T(8,128)(2,1)S(1)}, u32[]{:S(2)}, u32[]{:S(2)}) async-start(bf16[32,16,128]{2,1,0:T(8,128)(2,1)} %document_messages.1), calls=%async_computation.3 | async-start | bytes 262144 | tf_op jit(solution)/shard_map/all_to_all | solution.py:168
  115.9 0.0 collective-permute-done.7.refs_10_
  115.9 0.7 copy-done.10
  116.6 6.6 %input_gradient.1 = (bf16[8,128,256]{2,1,0:T(8,128)(2,1)}, bf16[8,128,256]{2,1,0:T(8,128)(2,1)}, bf16[8,128,256]{2,1,0:T(8,128)(2,1)}, bf16[8,128,256]{2,1,0:T(8,128)(2,1)}) custom-call(s32[5]{0:T(128)S(1)} %stack.23.place_ref, bf16[128,640]{1,0:T(8,128)(2,1)S(1)} %copy-done.1, bf16[128,640]{1,0:T(8,128)(2,1)S(1)} %collective-permute-done.refs_2_.refs_1_, ...), custom_call_target="tpu_custom_call" | custom-call | tf_op jit(solution)/shard_map/input_gradient/pallas_call | solution.py:245
  123.2 1.9 %collective-permute-start.13 = (bf16[8,128,256]{2,1,0:T(8,128)(2,1)}, bf16[8,128,256]{2,1,0:T(8,128)(2,1)S(1)}, u32[]{:S(2)}, u32[]{:S(2)}) collective-permute-start(bf16[8,128,256]{2,1,0:T(8,128)(2,1)} %get-tuple-element.20), channel_id=1, source_target_pairs={{0,1},{1,0},{2,3},{3,2},{4,5},{5,4},{6,7},{7,6},{8,9},{9,8},{10,11... | collective-permute-start | bytes 1572872 | tf_op jit(solution)/shard_map/ppermute | solution.py:173
  125.1 1.3 all-to-all-done.3.messages_ref
  126.5 0.8 clipped_sum.1
  127.2 3.5 %collective-permute-start.12 = (bf16[8,128,256]{2,1,0:T(8,128)(2,1)}, bf16[8,128,256]{2,1,0:T(8,128)(2,1)S(1)}, u32[]{:S(2)}, u32[]{:S(2)}) collective-permute-start(bf16[8,128,256]{2,1,0:T(8,128)(2,1)} %get-tuple-element.19), channel_id=1, source_target_pairs={{0,16},{16,0},{1,17},{17,1},{2,18},{18,2},{3,19},{19,3},{4,20},{20... | collective-permute-start | bytes 1572872 | tf_op jit(solution)/shard_map/ppermute | solution.py:173
  130.8 1.9 %collective-permute-start.14 = (bf16[8,128,256]{2,1,0:T(8,128)(2,1)}, bf16[8,128,256]{2,1,0:T(8,128)(2,1)S(1)}, u32[]{:S(2)}, u32[]{:S(2)}) collective-permute-start(bf16[8,128,256]{2,1,0:T(8,128)(2,1)} %get-tuple-element.21), channel_id=1, source_target_pairs={{0,17},{1,16},{16,1},{17,0},{2,19},{3,18},{18,3},{19,2},{4,21},{5,... | collective-permute-start | bytes 1572872 | tf_op jit(solution)/shard_map/ppermute | solution.py:173
  132.7 9.0 %all-to-all-start.4 = ((bf16[32,16,128]{2,1,0:T(8,128)(2,1)}), bf16[32,16,128]{2,1,0:T(8,128)(2,1)S(1)}, u32[]{:S(2)}, u32[]{:S(2)}) async-start(bf16[32,16,128]{2,1,0:T(8,128)(2,1)} %get-tuple-element.22), calls=%async_computation.4 | async-start | bytes 262144 | tf_op jit(solution)/shard_map/all_to_all | solution.py:168
  141.7 10.1 %collective-permute-done.14.refs_3_ = bf16[8,128,256]{2,1,0:T(8,128)(2,1)S(1)} collective-permute-done((bf16[8,128,256]{2,1,0:T(8,128)(2,1)}, bf16[8,128,256]{2,1,0:T(8,128)(2,1)S(1)}, u32[]{:S(2)}, u32[]{:S(2)}) %collective-permute-start.14) | collective-permute-done | bytes 524320 | tf_op jit(solution)/shard_map/ppermute | solution.py:173
  151.8 3.0 %interleave.1._ = bf16[128,8192]{1,0:T(8,128)(2,1)} custom-call(s32[5]{0:T(128)S(1)} %stack.23.place_ref, bf16[8,128,256]{2,1,0:T(8,128)(2,1)} %get-tuple-element.14.refs_0_, bf16[8,128,256]{2,1,0:T(8,128)(2,1)S(1)} %collective-permute-done.12.refs_1_, bf16[8,128,256]{2,1,0:T(8,128)(2,1)S(1)} %collective-permute-done.13.refs_2_, ...), custom_call_target="tpu_custom_call" | custom-call | tf_op jit(solution)/shard_map/interleave/pallas_call | solution.py:272
  154.8 0.8 finish.1
  (26 shorter events, 0.1 us)
Async XLA Ops:
  0.6 11.9 %copy-start = (bf16[256,640]{1,0:T(8,128)(2,1)S(1)}, bf16[256,640]{1,0:T(8,128)(2,1)}, u32[]{:S(2)}) copy-start(bf16[256,640]{1,0:T(8,128)(2,1)} %param.9) | copy-start | bytes 983044
  2.3 30.8 %all-to-all-start = ((bf16[16,64,256]{2,1,0:T(8,128)(2,1)}), bf16[16,64,256]{2,1,0:T(8,128)(2,1)S(1)}, u32[]{:S(2)}, u32[]{:S(2)}) async-start(bf16[16,64,256]{2,1,0:T(8,128)(2,1)} %copies.1), calls=%async_computation | async-start | bytes 1048576 | tf_op jit(solution)/shard_map/all_to_all | solution.py:168
  12.5 13.5 %collective-permute-start.3 = (bf16[128,640]{1,0:T(8,128)(2,1)S(1)}, bf16[128,640]{1,0:T(8,128)(2,1)S(1)}, u32[]{:S(2)}, u32[]{:S(2)}) collective-permute-start(bf16[128,640]{1,0:T(8,128)(2,1)S(1)} %constant_dynamic-slice_fusion.own_ref), channel_id=1, source_target_pairs={{0,256},{256,0},{1,257},{257,1},{2,258},{258,2},{3,259},{259,3},{4... | collective-permute-start | bytes 491528 | tf_op jit(solution)/shard_map/ppermute | solution.py:173
  17.3 12.9 %collective-permute-start.2 = (bf16[128,640]{1,0:T(8,128)(2,1)}, bf16[128,640]{1,0:T(8,128)(2,1)S(1)}, u32[]{:S(2)}, u32[]{:S(2)}) collective-permute-start(bf16[128,640]{1,0:T(8,128)(2,1)} %g_ref.1), channel_id=1, source_target_pairs={{0,17},{1,16},{16,1},{17,0},{2,19},{3,18},{18,3},{19,2},{4,21},{5,... | collective-permute-start | bytes 491528 | tf_op jit(solution)/shard_map/ppermute | solution.py:173
  21.0 12.1 %collective-permute-start.1 = (bf16[128,640]{1,0:T(8,128)(2,1)}, bf16[128,640]{1,0:T(8,128)(2,1)S(1)}, u32[]{:S(2)}, u32[]{:S(2)}) collective-permute-start(bf16[128,640]{1,0:T(8,128)(2,1)} %g_ref.1), channel_id=1, source_target_pairs={{0,1},{1,0},{2,3},{3,2},{4,5},{5,4},{6,7},{7,6},{8,9},{9,8},{10,11... | collective-permute-start | bytes 491528 | tf_op jit(solution)/shard_map/ppermute | solution.py:173
  24.0 9.0 %collective-permute-start = (bf16[128,640]{1,0:T(8,128)(2,1)}, bf16[128,640]{1,0:T(8,128)(2,1)S(1)}, u32[]{:S(2)}, u32[]{:S(2)}) collective-permute-start(bf16[128,640]{1,0:T(8,128)(2,1)} %g_ref.1), channel_id=1, source_target_pairs={{0,16},{16,0},{1,17},{17,1},{2,18},{18,2},{3,19},{19,3},{4,20},{20... | collective-permute-start | bytes 491528 | tf_op jit(solution)/shard_map/ppermute | solution.py:173
  33.1 4.3 %collective-permute-start.11 = (bf16[16,64,256]{2,1,0:T(8,128)(2,1)S(1)}, bf16[16,64,256]{2,1,0:T(8,128)(2,1)S(1)}, u32[]{:S(2)}, u32[]{:S(2)}) collective-permute-start(bf16[16,64,256]{2,1,0:T(8,128)(2,1)S(1)} %wait.1.refs_5_.own_ref), channel_id=1, source_target_pairs={{0,16},{16,0},{1,17},{17,1},{2,18},{18,2},{3,19},{19,3},{4,20},{20... | collective-permute-start | bytes 1572872 | tf_op jit(solution)/shard_map/ppermute | solution.py:173
  41.7 75.0 %copy-start.1 = (bf16[128,640]{1,0:T(8,128)(2,1)S(1)}, bf16[128,640]{1,0:T(8,128)(2,1)}, u32[]{:S(2)}) copy-start(bf16[128,640]{1,0:T(8,128)(2,1)} %g_ref.1) | copy-start | bytes 491524
  41.7 75.0 %copy-start.2 = (bf16[64,640]{1,0:T(8,128)(2,1)S(1)}, bf16[64,640]{1,0:T(8,128)(2,1)}, u32[]{:S(2)}) copy-start(bf16[64,640]{1,0:T(8,128)(2,1)} %b_ref.1) | copy-start | bytes 245764
  41.7 47.3 %all-to-all-start.1 = ((bf16[16,72,512]{2,1,0:T(8,128)(2,1)}), bf16[16,72,512]{2,1,0:T(8,128)(2,1)S(1)}, u32[]{:S(2)}, u32[]{:S(2)}) async-start(bf16[16,72,512]{2,1,0:T(8,128)(2,1)} %partials.1), calls=%async_computation.1 | async-start | bytes 2359296 | tf_op jit(solution)/shard_map/all_to_all | solution.py:168
  52.8 10.5 %collective-permute-start.8 = (bf16[2,128,640]{2,1,0:T(8,128)(2,1)S(1)}, bf16[2,128,640]{2,1,0:T(8,128)(2,1)S(1)}, u32[]{:S(2)}, u32[]{:S(2)}) collective-permute-start(bf16[2,128,640]{2,1,0:T(8,128)(2,1)S(1)} %own_rows.1.refs_1_.refs_6_), channel_id=1, source_target_pairs={{0,224},{32,0},{64,32},{96,64},{128,96},{160,128},{192,160},{224,1... | collective-permute-start | bytes 983048 | tf_op jit(solution)/shard_map/ppermute | solution.py:177
  56.8 11.7 %collective-permute-start.4 = (bf16[2,128,640]{2,1,0:T(8,128)(2,1)S(1)}, bf16[2,128,640]{2,1,0:T(8,128)(2,1)S(1)}, u32[]{:S(2)}, u32[]{:S(2)}) collective-permute-start(bf16[2,128,640]{2,1,0:T(8,128)(2,1)S(1)} %own_rows.1.refs_1_.refs_6_), channel_id=1, source_target_pairs={{0,32},{32,64},{64,96},{96,128},{128,160},{160,192},{192,224},{224... | collective-permute-start | bytes 983048 | tf_op jit(solution)/shard_map/ppermute | solution.py:177
  63.3 7.1 %copy-start.6 = (bf16[2,128,640]{2,1,0:T(8,128)(2,1)}, bf16[2,128,640]{2,1,0:T(8,128)(2,1)S(1)}, u32[]{:S(2)}) copy-start(bf16[2,128,640]{2,1,0:T(8,128)(2,1)S(1)} %collective-permute-done.8.refs_13_) | copy-start | bytes 983044
  63.3 10.6 %collective-permute-start.9 = (bf16[2,128,640]{2,1,0:T(8,128)(2,1)S(1)}, bf16[2,128,640]{2,1,0:T(8,128)(2,1)S(1)}, u32[]{:S(2)}, u32[]{:S(2)}) collective-permute-start(bf16[2,128,640]{2,1,0:T(8,128)(2,1)S(1)} %collective-permute-done.8.refs_13_), channel_id=1, source_target_pairs={{0,224},{32,0},{64,32},{96,64},{128,96},{160,128},{192,160},{224,1... | collective-permute-start | bytes 983048 | tf_op jit(solution)/shard_map/ppermute | solution.py:177
  68.5 15.3 %copy-start.7 = (bf16[2,128,640]{2,1,0:T(8,128)(2,1)}, bf16[2,128,640]{2,1,0:T(8,128)(2,1)S(1)}, u32[]{:S(2)}) copy-start(bf16[2,128,640]{2,1,0:T(8,128)(2,1)S(1)} %collective-permute-done.4.refs_7_) | copy-start | bytes 983044
  68.5 10.8 %collective-permute-start.5 = (bf16[2,128,640]{2,1,0:T(8,128)(2,1)S(1)}, bf16[2,128,640]{2,1,0:T(8,128)(2,1)S(1)}, u32[]{:S(2)}, u32[]{:S(2)}) collective-permute-start(bf16[2,128,640]{2,1,0:T(8,128)(2,1)S(1)} %collective-permute-done.4.refs_7_), channel_id=1, source_target_pairs={{0,32},{32,64},{64,96},{96,128},{128,160},{160,192},{192,224},{224... | collective-permute-start | bytes 983048 | tf_op jit(solution)/shard_map/ppermute | solution.py:177
  73.9 9.9 %copy-start.8 = (bf16[2,128,640]{2,1,0:T(8,128)(2,1)}, bf16[2,128,640]{2,1,0:T(8,128)(2,1)S(1)}, u32[]{:S(2)}) copy-start(bf16[2,128,640]{2,1,0:T(8,128)(2,1)S(1)} %collective-permute-done.9.refs_12_) | copy-start | bytes 983044
  73.9 9.8 %collective-permute-start.10 = (bf16[2,128,640]{2,1,0:T(8,128)(2,1)S(1)}, bf16[2,128,640]{2,1,0:T(8,128)(2,1)S(1)}, u32[]{:S(2)}, u32[]{:S(2)}) collective-permute-start(bf16[2,128,640]{2,1,0:T(8,128)(2,1)S(1)} %collective-permute-done.9.refs_12_), channel_id=1, source_target_pairs={{0,224},{32,0},{64,32},{96,64},{128,96},{160,128},{192,160},{224,1... | collective-permute-start | bytes 983048 | tf_op jit(solution)/shard_map/ppermute | solution.py:177
  79.2 4.5 %copy-start.9 = (bf16[2,128,640]{2,1,0:T(8,128)(2,1)}, bf16[2,128,640]{2,1,0:T(8,128)(2,1)S(1)}, u32[]{:S(2)}) copy-start(bf16[2,128,640]{2,1,0:T(8,128)(2,1)S(1)} %collective-permute-done.5.refs_8_) | copy-start | bytes 983044
  79.2 9.7 %collective-permute-start.6 = (bf16[2,128,640]{2,1,0:T(8,128)(2,1)S(1)}, bf16[2,128,640]{2,1,0:T(8,128)(2,1)}, u32[]{:S(2)}, u32[]{:S(2)}) collective-permute-start(bf16[2,128,640]{2,1,0:T(8,128)(2,1)S(1)} %collective-permute-done.5.refs_8_), channel_id=1, source_target_pairs={{0,32},{32,64},{64,96},{96,128},{128,160},{160,192},{192,224},{224... | collective-permute-start | bytes 983048 | tf_op jit(solution)/shard_map/ppermute | solution.py:177
  83.8 0.7 copy-start.5
  89.8 14.3 %all-to-all-start.2 = ((f32[16,8,128]{2,1,0:T(8,128)}), f32[16,8,128]{2,1,0:T(8,128)S(1)}, u32[]{:S(2)}, u32[]{:S(2)}) async-start(f32[16,8,128]{2,1,0:T(8,128)} %get-tuple-element.16), calls=%async_computation.2 | async-start | bytes 131072 | tf_op jit(solution)/shard_map/all_to_all | solution.py:168
  96.2 19.7 %collective-permute-start.7 = (bf16[2,128,640]{2,1,0:T(8,128)(2,1)}, bf16[2,128,640]{2,1,0:T(8,128)(2,1)S(1)}, u32[]{:S(2)}, u32[]{:S(2)}) collective-permute-start(bf16[2,128,640]{2,1,0:T(8,128)(2,1)} %collective-permute-done.6.refs_9_.up_ref), channel_id=1, source_target_pairs={{0,32},{32,64},{64,96},{96,128},{128,160},{160,192},{192,224},{224... | collective-permute-start | bytes 983048 | tf_op jit(solution)/shard_map/ppermute | solution.py:177
  104.8 21.7 %all-to-all-start.3 = ((bf16[32,16,128]{2,1,0:T(8,128)(2,1)}), bf16[32,16,128]{2,1,0:T(8,128)(2,1)S(1)}, u32[]{:S(2)}, u32[]{:S(2)}) async-start(bf16[32,16,128]{2,1,0:T(8,128)(2,1)} %document_messages.1), calls=%async_computation.3 | async-start | bytes 262144 | tf_op jit(solution)/shard_map/all_to_all | solution.py:168
  115.9 0.7 copy-start.10
  123.2 18.5 %collective-permute-start.13 = (bf16[8,128,256]{2,1,0:T(8,128)(2,1)}, bf16[8,128,256]{2,1,0:T(8,128)(2,1)S(1)}, u32[]{:S(2)}, u32[]{:S(2)}) collective-permute-start(bf16[8,128,256]{2,1,0:T(8,128)(2,1)} %get-tuple-element.20), channel_id=1, source_target_pairs={{0,1},{1,0},{2,3},{3,2},{4,5},{5,4},{6,7},{7,6},{8,9},{9,8},{10,11... | collective-permute-start | bytes 1572872 | tf_op jit(solution)/shard_map/ppermute | solution.py:173
  127.2 14.5 %collective-permute-start.12 = (bf16[8,128,256]{2,1,0:T(8,128)(2,1)}, bf16[8,128,256]{2,1,0:T(8,128)(2,1)S(1)}, u32[]{:S(2)}, u32[]{:S(2)}) collective-permute-start(bf16[8,128,256]{2,1,0:T(8,128)(2,1)} %get-tuple-element.19), channel_id=1, source_target_pairs={{0,16},{16,0},{1,17},{17,1},{2,18},{18,2},{3,19},{19,3},{4,20},{20... | collective-permute-start | bytes 1572872 | tf_op jit(solution)/shard_map/ppermute | solution.py:173
  130.8 21.0 %collective-permute-start.14 = (bf16[8,128,256]{2,1,0:T(8,128)(2,1)}, bf16[8,128,256]{2,1,0:T(8,128)(2,1)S(1)}, u32[]{:S(2)}, u32[]{:S(2)}) collective-permute-start(bf16[8,128,256]{2,1,0:T(8,128)(2,1)} %get-tuple-element.21), channel_id=1, source_target_pairs={{0,17},{1,16},{16,1},{17,0},{2,19},{3,18},{18,3},{19,2},{4,21},{5,... | collective-permute-start | bytes 1572872 | tf_op jit(solution)/shard_map/ppermute | solution.py:173
  132.7 22.1 %all-to-all-start.4 = ((bf16[32,16,128]{2,1,0:T(8,128)(2,1)}), bf16[32,16,128]{2,1,0:T(8,128)(2,1)S(1)}, u32[]{:S(2)}, u32[]{:S(2)}) async-start(bf16[32,16,128]{2,1,0:T(8,128)(2,1)} %get-tuple-element.22), calls=%async_computation.4 | async-start | bytes 262144 | tf_op jit(solution)/shard_map/all_to_all | solution.py:168
  151.8 3.0 %copy-start.3 = (f32[512,64]{0,1:T(8,128)S(1)}, f32[512,64]{0,1:T(8,128)}, u32[]{:S(2)}) copy-start(f32[512,64]{0,1:T(8,128)} %param.12) | copy-start | bytes 393220
  151.8 3.0 %copy-start.4 = (f32[64,40]{0,1:T(8,128)S(1)}, f32[64,40]{0,1:T(8,128)}, u32[]{:S(2)}) copy-start(f32[64,40]{0,1:T(8,128)} %param.13) | copy-start | bytes 30724
